TPU v7x, 1024 devices: a whole 8x8x8 slice. The times are simulated.
1024 devices in a mesh: sec: 4 (over x_lo), tile: 128 (over y, z, core), col: 2 (over x_hi).
Axes of the slice: x: 8 (x_hi: 2, x_lo: 4; x = x_hi * 4 + x_lo), y: 8, z: 8, core: 2. Of those that a mesh axis runs over, the one named last changes fastest.
Arguments:
- state: float32 [4, 8, 72, 256, 256], P('sec', None, None, 'tile', 'col'), may hold values from -6 to 6
- column_op: bfloat16 [4, 576, 576], P('sec'), may hold values from -0.125 to 0.125
- diffusion: float32 [4, 576], P('sec'), may hold values from 0.05 to 0.22
- remap_weights: bfloat16 [32, 128, 128], replicated, may hold values from -0.5 to 0.5
- source_rows: int32 [4, 256, 2, 4], P('sec', 'tile', 'col'), may hold values from 0 to 23, as said below
- weight_index: int32 [4, 256, 2, 4], P('sec', 'tile', 'col'), may hold values from 0 to 31
- intersection_count: int32 [4, 256, 2], P('sec', 'tile', 'col'), may hold values from 1 to 4, as said below
Outputs:
- state_next: float32 [4, 8, 72, 256, 256], P('sec', None, None, 'tile', 'col')
Inputs may be any that keep to these rules, and one draw needn't show every extreme that they name: `source_rows`: each entry is s * 3 * 2 + (d + 1) * 2 + r for a source section s, a tile offset d of -1, 0 or 1 and a row r; blocks of the atmosphere sections (all but the last) take their sources from the last section only, blocks of the last section from the others only. Slots 0 to intersection_count - 1 of a block's list are live; every device holds a block with 4 live slots.
All inputs are finite; a program needn't handle non-finite values.
Results may differ from a plain program's by a relative error of at most 0.0017.
Values may be sent and summed in bfloat16 or wider, within the bound.
No kernel may reach another device: no remote copies, remote signals or barrier semaphores. Data moves between devices by JAX's collectives and lax.ppermute only.
A program may use at most 32 MiB of HBM per device.

v0:
```python
import jax
import jax.numpy as jnp
from jax import lax
from jax.sharding import PartitionSpec as P

SUBSTEPS = 2


def with_halo(cells, sides, width):
    for axis, dim in sides:
        count = lax.axis_size(axis)
        head = lax.slice_in_dim(cells, 0, width, axis=dim)
        tail = lax.slice_in_dim(cells, cells.shape[dim] - width, cells.shape[dim], axis=dim)
        cells = jnp.concatenate(
            [
                lax.ppermute(tail, axis, [(i, (i + 1) % count) for i in range(count)]),
                cells,
                lax.ppermute(head, axis, [((i + 1) % count, i) for i in range(count)]),
            ],
            axis=dim,
        )
    return cells


def physics(field, operator):
    dims_now = field.shape
    rounded = field.astype(jnp.bfloat16).reshape(
        dims_now[0] * dims_now[1], dims_now[2] * dims_now[3]
    )
    tendency = jnp.dot(operator, rounded, preferred_element_type=jnp.float32)
    return field + tendency.reshape(dims_now)


def stencil_step(padded, spread_rate, operator):
    center = padded[:, :, 1:-1, 1:-1]
    laplace = (
        padded[:, :, 2:, 1:-1]
        + padded[:, :, :-2, 1:-1]
        + padded[:, :, 1:-1, 2:]
        + padded[:, :, 1:-1, :-2]
        - 4.0 * center
    )
    return physics(center + spread_rate * laplace, operator)


def shards(
    state, column_op, diffusion, remap_weights, source_rows, weight_index, intersection_count
):
    field = state[0]
    num_vars, num_levels, num_rows, num_cells = field.shape
    operator = column_op[0]
    spread_rate = diffusion[0].reshape(num_vars, num_levels, 1, 1)
    surface = jnp.moveaxis(field[:, 0], 1, 0).astype(jnp.bfloat16)
    nearby = with_halo(surface, (("tile", 0),), num_rows)
    table = lax.all_gather(nearby, "sec", axis=0, tiled=True)
    entries = source_rows[0, :, 0, :]
    picks = weight_index[0, :, 0, :]
    counts = intersection_count[0, :, 0]
    flux = jnp.zeros((num_rows, num_vars, num_cells), jnp.float32)
    for slot_index in range(entries.shape[1]):
        blocks = table[entries[:, slot_index]]
        weights = remap_weights[picks[:, slot_index]]
        contrib = jnp.einsum("rvi,rij->rvj", blocks, weights, preferred_element_type=jnp.float32)
        live = (slot_index < counts)[:, None, None]
        flux = flux + jnp.where(live, contrib, jnp.float32(0.0))
    for substep in range(SUBSTEPS):
        padded = with_halo(field, (("tile", 2), ("col", 3)), 1)
        field = stencil_step(padded, spread_rate, operator)
    field = field.at[:, 0].add(0.5 * jnp.moveaxis(flux, 0, 1))
    return field[None]


def solution(mesh):
    in_specs = (
        P("sec", None, None, "tile", "col"),
        P("sec", None, None),
        P("sec", None),
        P(),
        P("sec", "tile", "col", None),
        P("sec", "tile", "col", None),
        P("sec", "tile", "col"),
    )
    out_specs = P("sec", None, None, "tile", "col")
    return jax.shard_map(shards, mesh=mesh, in_specs=in_specs, out_specs=out_specs, check_vma=False)
```

profile of v0, /device:TPU:14, one launch (start us, length us, event | category | flops | bytes accessed | tf_op | source)
XLA Modules:
  0.0 125.2 jit_solution(17202266674001814923)
XLA Ops:
  0.0 1.3 %copy.48 = f32[1,8,72,2,128]{4,1,3,2,0:T(8,128)S(1)} copy(f32[1,8,72,2,128]{4,3,2,1,0:T(2,128)} %param.9) | data formatting | bytes 1179648 | tf_op args[0]
  1.4 20.5 %collective-permute-start.9 = (bf16[2,8,128]{2,1,0:T(8,128)(2,1)S(1)}, bf16[2,8,128]{2,1,0:T(8,128)(2,1)S(1)}, u32[]{:S(2)}, u32[]{:S(2)}) collective-permute-start(bf16[2,8,128]{2,1,0:T(8,128)(2,1)S(1)} %fusion.26), channel_id=1, source_target_pairs={{2,0},{4,2},{6,4},{8,6},{10,8},{12,10},{14,12},{16,14},{18,16},{20... | collective-permute-start | bytes 12296 | tf_op jit(solution)/shard_map/ppermute | solution.py:18
  21.8 1.9 %collective-permute-start.8 = (bf16[2,8,128]{2,1,0:T(8,128)(2,1)S(1)}, bf16[2,8,128]{2,1,0:T(8,128)(2,1)S(1)}, u32[]{:S(2)}, u32[]{:S(2)}) collective-permute-start(bf16[2,8,128]{2,1,0:T(8,128)(2,1)S(1)} %fusion.26), channel_id=1, source_target_pairs={{0,2},{2,4},{4,6},{6,8},{8,10},{10,12},{12,14},{14,16},{16,18},{18... | collective-permute-start | bytes 12296 | tf_op jit(solution)/shard_map/ppermute | solution.py:16
  23.8 1.9 %collective-permute-start.1 = (f32[8,72,1,128]{3,0,2,1:T(8,128)S(1)}, f32[8,72,1,128]{3,0,2,1:T(8,128)S(1)}, u32[]{:S(2)}, u32[]{:S(2)}) collective-permute-start(f32[8,72,1,128]{3,0,2,1:T(8,128)S(1)} %get-tuple-element.35), channel_id=1, source_target_pairs={{0,2},{2,4},{4,6},{6,8},{8,10},{10,12},{12,14},{14,16},{16,18},{18... | collective-permute-start | bytes 884744 | tf_op jit(solution)/shard_map/ppermute | solution.py:16
  25.8 7.0 %collective-permute-start = (f32[8,72,1,128]{3,0,2,1:T(8,128)S(1)}, f32[8,72,1,128]{3,0,2,1:T(8,128)S(1)}, u32[]{:S(2)}, u32[]{:S(2)}) collective-permute-start(f32[8,72,1,128]{3,0,2,1:T(8,128)S(1)} %get-tuple-element.36), channel_id=1, source_target_pairs={{2,0},{4,2},{6,4},{8,6},{10,8},{12,10},{14,12},{16,14},{18,16},{20... | collective-permute-start | bytes 884744 | tf_op jit(solution)/shard_map/ppermute | solution.py:18
  35.8 1.2 gather_fusion.5
  37.0 1.2 gather_fusion.1
  38.2 1.2 gather_fusion.7
  39.4 1.2 gather_fusion.3
  42.1 1.5 %fusion.40 = (f32[8,72,4,1]{3,0,2,1:T(8,128)}, f32[8,72,4,1]{3,0,2,1:T(8,128)S(1)}) fusion(f32[8,72,4,128]{3,0,2,1:T(8,128)S(1)} %pad_maximum_fusion), kind=kLoop, calls=%fused_computation.95 | loop fusion | bytes 36864 | tf_op jit(solution)/shard_map/slice | solution.py:12
  43.6 1.9 %copy.22 = f32[8,72,4,1]{1,0,3,2:T(8,128)S(1)} copy(f32[8,72,4,1]{3,0,2,1:T(8,128)} %get-tuple-element.31) | data formatting | bytes 18432 | tf_op jit(solution)/shard_map/slice | solution.py:12
  46.2 5.0 %collective-permute-start.3 = (f32[8,72,4,1]{1,0,3,2:T(8,128)S(1)}, f32[8,72,4,1]{1,0,3,2:T(8,128)S(1)}, u32[]{:S(2)}, u32[]{:S(2)}) collective-permute-start(f32[8,72,4,1]{1,0,3,2:T(8,128)S(1)} %copy.24), channel_id=1, source_target_pairs={{0,1},{1,0},{2,3},{3,2},{4,5},{5,4},{6,7},{7,6},{8,9},{9,8},{10,11... | collective-permute-start | bytes 27656 | tf_op jit(solution)/shard_map/ppermute | solution.py:16
  51.2 4.7 %collective-permute-start.2 = (f32[8,72,4,1]{1,0,3,2:T(8,128)S(1)}, f32[8,72,4,1]{1,0,3,2:T(8,128)S(1)}, u32[]{:S(2)}, u32[]{:S(2)}) collective-permute-start(f32[8,72,4,1]{1,0,3,2:T(8,128)S(1)} %copy.22), channel_id=1, source_target_pairs={{1,0},{0,1},{3,2},{2,3},{5,4},{4,5},{7,6},{6,7},{9,8},{8,9},{11,10... | collective-permute-start | bytes 27656 | tf_op jit(solution)/shard_map/ppermute | solution.py:18
  55.9 13.1 %all_gather.3 = bf16[24,8,128]{2,1,0:T(8,128)(2,1)S(1)} all-gather(bf16[6,8,128]{2,1,0:T(8,128)(2,1)S(1)} %pad_maximum_fusion.18), channel_id=1, replica_groups=mesh['sec'=4,'tile'=128,'col'=2] {'sec'}, dimensions={0}, use_global_device_ids=true | all-gather | bytes 61440 | tf_op jit(solution)/shard_map/all_gather | solution.py:55
  71.3 2.0 %copy.25 = f32[8,72,4,1]{3,0,2,1:T(8,128)} copy(f32[8,72,4,1]{1,0,3,2:T(8,128)S(1)} %collective-permute-done.3) | data formatting | bytes 18432 | tf_op jit(solution)/shard_map/ppermute | solution.py:16
  73.3 2.7 %fusion.37 = (bf16[8,72,2,128]{3,0,2,1:T(8,128)(2,1)S(1)}, f32[8,72,2,128]{3,0,2,1:T(8,128)}) fusion(f32[8,72,2,128]{3,0,2,1:T(8,128)S(1)} %bitcast.62, f32[8,72,1,128]{3,0,2,1:T(8,128)} %copy-done.5, f32[8,72,1,128]{3,0,2,1:T(8,128)} %copy-done.4, f32[8,72,4,1]{3,0,2,1:T(8,128)} %copy.25, f32[8,72,4,1]{3,0,2,1:T(8,128)S(1)} %copy.23, f32[8,72]{0,1:T(8,128)} %copy.21), kind=kLoop, calls=%fused_computation.93 | loop fusion | flops 2359296 | bytes 2085120 | tf_op jit(solution)/shard_map/convert_element_type | solution.py:27
  77.6 1.9 %collective-permute-start.5 = (f32[8,72,1,128]{3,0,2,1:T(8,128)S(1)}, f32[8,72,1,128]{3,0,2,1:T(8,128)S(1)}, u32[]{:S(2)}, u32[]{:S(2)}) collective-permute-start(f32[8,72,1,128]{3,0,2,1:T(8,128)S(1)} %get-tuple-element.33), channel_id=1, source_target_pairs={{0,2},{2,4},{4,6},{6,8},{8,10},{10,12},{12,14},{14,16},{16,18},{18... | collective-permute-start | bytes 884744 | tf_op jit(solution)/shard_map/ppermute | solution.py:16
  79.5 7.0 %collective-permute-start.4 = (f32[8,72,1,128]{3,0,2,1:T(8,128)S(1)}, f32[8,72,1,128]{3,0,2,1:T(8,128)S(1)}, u32[]{:S(2)}, u32[]{:S(2)}) collective-permute-start(f32[8,72,1,128]{3,0,2,1:T(8,128)S(1)} %get-tuple-element.34), channel_id=1, source_target_pairs={{2,0},{4,2},{6,4},{8,6},{10,8},{12,10},{14,12},{16,14},{18,16},{20... | collective-permute-start | bytes 884744 | tf_op jit(solution)/shard_map/ppermute | solution.py:18
  87.2 2.1 %gather_fusion.4 = bf16[2,8,128]{2,1,0:T(8,128)(2,1)} fusion(bf16[24,8,128]{2,1,0:T(8,128)(2,1)} %copy-done.10, s32[1024]{0:T(1024)} %get-tuple-element.41), kind=kCustom, calls=%fused_computation.4 | custom fusion | bytes 8200 | tf_op jit(solution)/shard_map/gather | solution.py:61
  89.3 2.1 %gather_fusion.2 = bf16[2,8,128]{2,1,0:T(8,128)(2,1)} fusion(bf16[24,8,128]{2,1,0:T(8,128)(2,1)} %copy-done.10, s32[1024]{0:T(1024)} %get-tuple-element.42), kind=kCustom, calls=%fused_computation.2 | custom fusion | bytes 8200 | tf_op jit(solution)/shard_map/gather | solution.py:61
  91.4 1.6 %fusion.7 = f32[2,8,128]{2,1,0:T(8,128)} fusion(f32[2,8,128]{2,1,0:T(8,128)} %convolution_select_fusion.3, bf16[2,8,128]{2,1,0:T(8,128)(2,1)} %gather_fusion.2, bf16[2,128,128]{2,1,0:T(8,128)(2,1)} %gather_fusion.3, pred[2]{0:T(512)(128)(4,1)} %get-tuple-element.38), kind=kOutput, calls=%fused_computation.22 | convolution fusion | flops 528384 | bytes 86018 | tf_op jit(solution)/shard_map/rvi,rij->rvj/dot_general | solution.py:63
  94.5 1.5 %fusion.39 = (f32[8,72,4,1]{3,0,2,1:T(8,128)}, f32[8,72,4,1]{3,0,2,1:T(8,128)S(1)}) fusion(f32[8,72,4,128]{3,0,2,1:T(8,128)S(1)} %pad_maximum_fusion.1), kind=kLoop, calls=%fused_computation.94 | loop fusion | bytes 36864 | tf_op jit(solution)/shard_map/slice | solution.py:12
  95.9 2.5 %copy.28 = f32[8,72,4,1]{1,0,3,2:T(8,128)} copy(f32[8,72,4,1]{3,0,2,1:T(8,128)} %get-tuple-element.29) | data formatting | bytes 18432 | tf_op jit(solution)/shard_map/slice | solution.py:12
  98.4 1.3 %copy.30 = f32[8,72,4,1]{1,0,3,2:T(8,128)} copy(f32[8,72,4,1]{3,0,2,1:T(8,128)S(1)} %get-tuple-element.30) | data formatting | bytes 18432 | tf_op jit(solution)/shard_map/slice | solution.py:13
  99.7 5.0 %collective-permute-start.7 = (f32[8,72,4,1]{1,0,3,2:T(8,128)}, f32[8,72,4,1]{1,0,3,2:T(8,128)}, u32[]{:S(2)}, u32[]{:S(2)}) collective-permute-start(f32[8,72,4,1]{1,0,3,2:T(8,128)} %copy.30), channel_id=1, source_target_pairs={{0,1},{1,0},{2,3},{3,2},{4,5},{5,4},{6,7},{7,6},{8,9},{9,8},{10,11... | collective-permute-start | bytes 27656 | tf_op jit(solution)/shard_map/ppermute | solution.py:16
  104.8 4.9 %collective-permute-start.6 = (f32[8,72,4,1]{1,0,3,2:T(8,128)}, f32[8,72,4,1]{1,0,3,2:T(8,128)}, u32[]{:S(2)}, u32[]{:S(2)}) collective-permute-start(f32[8,72,4,1]{1,0,3,2:T(8,128)} %copy.28), channel_id=1, source_target_pairs={{1,0},{0,1},{3,2},{2,3},{5,4},{4,5},{7,6},{6,7},{9,8},{8,9},{11,10... | collective-permute-start | bytes 27656 | tf_op jit(solution)/shard_map/ppermute | solution.py:18
  109.7 1.6 %fusion.6 = f32[2,8,128]{2,1,0:T(8,128)} fusion(f32[2,8,128]{2,1,0:T(8,128)} %fusion.7, bf16[2,8,128]{2,1,0:T(8,128)(2,1)} %gather_fusion.4, bf16[2,128,128]{2,1,0:T(8,128)(2,1)} %gather_fusion.5, pred[2]{0:T(512)(128)(4,1)} %get-tuple-element.40), kind=kOutput, calls=%fused_computation.20 | convolution fusion | flops 528384 | bytes 86018 | tf_op jit(solution)/shard_map/rvi,rij->rvj/dot_general | solution.py:63
  111.2 2.1 %gather_fusion.6 = bf16[2,8,128]{2,1,0:T(8,128)(2,1)} fusion(bf16[24,8,128]{2,1,0:T(8,128)(2,1)} %copy-done.10, s32[1024]{0:T(1024)} %pad_clamp_fusion.1), kind=kCustom, calls=%fused_computation.6 | custom fusion | bytes 8200 | tf_op jit(solution)/shard_map/gather | solution.py:61
  113.3 1.3 %collective-permute-done.6 = f32[8,72,4,1]{1,0,3,2:T(8,128)} collective-permute-done((f32[8,72,4,1]{1,0,3,2:T(8,128)}, f32[8,72,4,1]{1,0,3,2:T(8,128)}, u32[]{:S(2)}, u32[]{:S(2)}) %collective-permute-start.6) | collective-permute-done | bytes 9248 | tf_op jit(solution)/shard_map/ppermute | solution.py:18
  114.6 1.8 %copy.29 = f32[8,72,4,1]{3,0,2,1:T(8,128)S(1)} copy(f32[8,72,4,1]{1,0,3,2:T(8,128)} %collective-permute-done.6) | data formatting | bytes 18432 | tf_op jit(solution)/shard_map/ppermute | solution.py:18
  116.4 2.7 %copy.31 = f32[8,72,4,1]{3,0,2,1:T(8,128)} copy(f32[8,72,4,1]{1,0,3,2:T(8,128)} %collective-permute-done.7) | data formatting | bytes 18432 | tf_op jit(solution)/shard_map/ppermute | solution.py:16
  119.1 2.7 %fusion.35 = (bf16[8,72,2,128]{3,0,2,1:T(8,128)(2,1)S(1)}, f32[8,72,2,128]{3,0,2,1:T(8,128)}) fusion(f32[8,72,2,128]{3,0,2,1:T(8,128)S(1)} %copy_add_fusion.1, f32[8,72,1,128]{3,0,2,1:T(8,128)} %copy-done.7, f32[8,72,1,128]{3,0,2,1:T(8,128)} %copy-done.6, f32[8,72,4,1]{3,0,2,1:T(8,128)} %copy.31, f32[8,72,4,1]{3,0,2,1:T(8,128)S(1)} %copy.29, f32[8,72]{0,1:T(8,128)} %copy.21), kind=kLoop, calls=%fused_computation.92 | loop fusion | flops 2359296 | bytes 2085120 | tf_op jit(solution)/shard_map/convert_element_type | solution.py:27
  (82 shorter events, 14.8 us)
Async XLA Ops:
  0.0 35.8 %copy-start = (bf16[32,128,128]{2,1,0:T(8,128)(2,1)S(1)}, bf16[32,128,128]{2,1,0:T(8,128)(2,1)}, u32[]{:S(2)}) copy-start(bf16[32,128,128]{2,1,0:T(8,128)(2,1)} %param.12) | copy-start | bytes 3145732
  0.0 32.7 %copy-start.14 = (s32[1,2,1,4]{3,2,1,0:T(1,128)S(1)}, s32[1,2,1,4]{3,2,1,0:T(1,128)}, u32[]{:S(2)}) copy-start(s32[1,2,1,4]{3,2,1,0:T(1,128)} %param.13) | copy-start | bytes 100
  0.0 32.9 %copy-start.15 = (s32[1,2,1,4]{3,2,1,0:T(1,128)S(1)}, s32[1,2,1,4]{3,2,1,0:T(1,128)}, u32[]{:S(2)}) copy-start(s32[1,2,1,4]{3,2,1,0:T(1,128)} %param.14) | copy-start | bytes 100
  0.0 33.2 %copy-start.19 = (s32[1,2,1]{1,2,0:T(1,128)S(1)}, s32[1,2,1]{1,2,0:T(1,128)}, u32[]{:S(2)}) copy-start(s32[1,2,1]{1,2,0:T(1,128)} %param.15) | copy-start | bytes 28
  0.0 35.0 %copy-start.16 = (f32[1,576]{1,0:T(1,128)S(1)}, f32[1,576]{1,0:T(1,128)}, u32[]{:S(2)}) copy-start(f32[1,576]{1,0:T(1,128)} %param.11) | copy-start | bytes 6916
  1.4 39.2 %collective-permute-start.9 = (bf16[2,8,128]{2,1,0:T(8,128)(2,1)S(1)}, bf16[2,8,128]{2,1,0:T(8,128)(2,1)S(1)}, u32[]{:S(2)}, u32[]{:S(2)}) collective-permute-start(bf16[2,8,128]{2,1,0:T(8,128)(2,1)S(1)} %fusion.26), channel_id=1, source_target_pairs={{2,0},{4,2},{6,4},{8,6},{10,8},{12,10},{14,12},{16,14},{18,16},{20... | collective-permute-start | bytes 12296 | tf_op jit(solution)/shard_map/ppermute | solution.py:18
  21.8 18.7 %collective-permute-start.8 = (bf16[2,8,128]{2,1,0:T(8,128)(2,1)S(1)}, bf16[2,8,128]{2,1,0:T(8,128)(2,1)S(1)}, u32[]{:S(2)}, u32[]{:S(2)}) collective-permute-start(bf16[2,8,128]{2,1,0:T(8,128)(2,1)S(1)} %fusion.26), channel_id=1, source_target_pairs={{0,2},{2,4},{4,6},{6,8},{8,10},{10,12},{12,14},{14,16},{16,18},{18... | collective-permute-start | bytes 12296 | tf_op jit(solution)/shard_map/ppermute | solution.py:16
  23.8 16.7 %collective-permute-start.1 = (f32[8,72,1,128]{3,0,2,1:T(8,128)S(1)}, f32[8,72,1,128]{3,0,2,1:T(8,128)S(1)}, u32[]{:S(2)}, u32[]{:S(2)}) collective-permute-start(f32[8,72,1,128]{3,0,2,1:T(8,128)S(1)} %get-tuple-element.35), channel_id=1, source_target_pairs={{0,2},{2,4},{4,6},{6,8},{8,10},{10,12},{12,14},{14,16},{16,18},{18... | collective-permute-start | bytes 884744 | tf_op jit(solution)/shard_map/ppermute | solution.py:16
  25.8 14.8 %collective-permute-start = (f32[8,72,1,128]{3,0,2,1:T(8,128)S(1)}, f32[8,72,1,128]{3,0,2,1:T(8,128)S(1)}, u32[]{:S(2)}, u32[]{:S(2)}) collective-permute-start(f32[8,72,1,128]{3,0,2,1:T(8,128)S(1)} %get-tuple-element.36), channel_id=1, source_target_pairs={{2,0},{4,2},{6,4},{8,6},{10,8},{12,10},{14,12},{16,14},{18,16},{20... | collective-permute-start | bytes 884744 | tf_op jit(solution)/shard_map/ppermute | solution.py:18
  40.6 0.7 copy-start.4
  41.3 0.7 copy-start.5
  46.2 25.1 %collective-permute-start.3 = (f32[8,72,4,1]{1,0,3,2:T(8,128)S(1)}, f32[8,72,4,1]{1,0,3,2:T(8,128)S(1)}, u32[]{:S(2)}, u32[]{:S(2)}) collective-permute-start(f32[8,72,4,1]{1,0,3,2:T(8,128)S(1)} %copy.24), channel_id=1, source_target_pairs={{0,1},{1,0},{2,3},{3,2},{4,5},{5,4},{6,7},{7,6},{8,9},{9,8},{10,11... | collective-permute-start | bytes 27656 | tf_op jit(solution)/shard_map/ppermute | solution.py:16
  51.2 18.9 %collective-permute-start.2 = (f32[8,72,4,1]{1,0,3,2:T(8,128)S(1)}, f32[8,72,4,1]{1,0,3,2:T(8,128)S(1)}, u32[]{:S(2)}, u32[]{:S(2)}) collective-permute-start(f32[8,72,4,1]{1,0,3,2:T(8,128)S(1)} %copy.22), channel_id=1, source_target_pairs={{1,0},{0,1},{3,2},{2,3},{5,4},{4,5},{7,6},{6,7},{9,8},{8,9},{11,10... | collective-permute-start | bytes 27656 | tf_op jit(solution)/shard_map/ppermute | solution.py:18
  69.0 1.1 copy-start.10
  73.3 3.0 %copy-start.1 = (bf16[1,576,576]{2,1,0:T(8,128)(2,1)S(1)}, bf16[1,576,576]{2,1,0:T(8,128)(2,1)}, u32[]{:S(2)}) copy-start(bf16[1,576,576]{2,1,0:T(8,128)(2,1)} %param.10) | copy-start | bytes 1990660
  76.2 1.1 copy-start.3
  77.3 9.2 %copy-start.9 = (bf16[2,128,128]{2,1,0:T(8,128)(2,1)S(1)}, bf16[2,128,128]{2,1,0:T(8,128)(2,1)}, u32[]{:S(2)}) copy-start(bf16[2,128,128]{2,1,0:T(8,128)(2,1)} %gather_fusion.1) | copy-start | bytes 196612
  77.3 9.2 %copy-start.12 = (bf16[2,8,128]{2,1,0:T(8,128)(2,1)S(1)}, bf16[2,8,128]{2,1,0:T(8,128)(2,1)}, u32[]{:S(2)}) copy-start(bf16[2,8,128]{2,1,0:T(8,128)(2,1)} %gather_fusion) | copy-start | bytes 12292
  77.3 9.2 %copy-start.18 = (pred[2]{0:T(512)(128)(4,1)S(1)}, pred[2]{0:T(512)(128)(4,1)}, u32[]{:S(2)}) copy-start(pred[2]{0:T(512)(128)(4,1)} %get-tuple-element.39) | copy-start | bytes 10
  77.6 15.4 %collective-permute-start.5 = (f32[8,72,1,128]{3,0,2,1:T(8,128)S(1)}, f32[8,72,1,128]{3,0,2,1:T(8,128)S(1)}, u32[]{:S(2)}, u32[]{:S(2)}) collective-permute-start(f32[8,72,1,128]{3,0,2,1:T(8,128)S(1)} %get-tuple-element.33), channel_id=1, source_target_pairs={{0,2},{2,4},{4,6},{6,8},{8,10},{10,12},{12,14},{14,16},{16,18},{18... | collective-permute-start | bytes 884744 | tf_op jit(solution)/shard_map/ppermute | solution.py:16
  79.5 13.4 %collective-permute-start.4 = (f32[8,72,1,128]{3,0,2,1:T(8,128)S(1)}, f32[8,72,1,128]{3,0,2,1:T(8,128)S(1)}, u32[]{:S(2)}, u32[]{:S(2)}) collective-permute-start(f32[8,72,1,128]{3,0,2,1:T(8,128)S(1)} %get-tuple-element.34), channel_id=1, source_target_pairs={{2,0},{4,2},{6,4},{8,6},{10,8},{12,10},{14,12},{16,14},{18,16},{20... | collective-permute-start | bytes 884744 | tf_op jit(solution)/shard_map/ppermute | solution.py:18
  92.9 0.7 copy-start.6
  93.6 0.7 copy-start.7
  99.7 16.7 %collective-permute-start.7 = (f32[8,72,4,1]{1,0,3,2:T(8,128)}, f32[8,72,4,1]{1,0,3,2:T(8,128)}, u32[]{:S(2)}, u32[]{:S(2)}) collective-permute-start(f32[8,72,4,1]{1,0,3,2:T(8,128)} %copy.30), channel_id=1, source_target_pairs={{0,1},{1,0},{2,3},{3,2},{4,5},{5,4},{6,7},{7,6},{8,9},{9,8},{10,11... | collective-permute-start | bytes 27656 | tf_op jit(solution)/shard_map/ppermute | solution.py:16
  104.8 9.9 %collective-permute-start.6 = (f32[8,72,4,1]{1,0,3,2:T(8,128)}, f32[8,72,4,1]{1,0,3,2:T(8,128)}, u32[]{:S(2)}, u32[]{:S(2)}) collective-permute-start(f32[8,72,4,1]{1,0,3,2:T(8,128)} %copy.28), channel_id=1, source_target_pairs={{1,0},{0,1},{3,2},{2,3},{5,4},{4,5},{7,6},{6,7},{9,8},{8,9},{11,10... | collective-permute-start | bytes 27656 | tf_op jit(solution)/shard_map/ppermute | solution.py:18
  122.0 1.1 copy-start.2
  123.1 0.8 copy-start.8
  123.1 0.8 copy-start.11
  123.1 0.8 copy-start.13
  123.1 0.8 copy-start.17
where the time goes:
time: 127 us; the launch traced here: 125 us
  starting transfers between devices  59.8 us (47%)
  local copies, waits for them, and re-layouts  37.5 us (30%)
  blocking collectives  13.1 us (10%)
  other arithmetic  8.31 us (7%)
  matrix products  4.78 us (4%)
  waiting for transfers between devices  1.36 us (1%)
    ppermute x5, starting transfers between devices, with_halo(): lax.ppermute(head, axis, [((i + 1) % count, i) for i in range(count)])  44 us
    ppermute x5, starting transfers between devices, with_halo(): lax.ppermute(tail, axis, [(i, (i + 1) % count) for i in range(count)])  15.9 us
    all_gather x1, blocking collectives, shards(): table = lax.all_gather(nearby, 'sec', axis=0, tiled=True)  13.1 us
    gather x4, local copies, waits for them, and re-layouts, shards(): blocks = table[entries[:, slot_index]]  7.33 us
    slice x4, local copies, waits for them, and re-layouts, with_halo(): head = lax.slice_in_dim(cells, 0, width, axis=dim)  7.28 us
    unnamed x42, local copies, waits for them, and re-layouts  5.53 us
    convert_element_type x2, other arithmetic, physics(): field.astype(jnp.bfloat16)  5.43 us
    gather x4, local copies, waits for them, and re-layouts, shards(): weights = remap_weights[picks[:, slot_index]]  4.73 us
  transfers between devices with their start and end apart: 10, of which 1 were waited for; matrix products, arithmetic and copies ran while one was open for 17% of the time, Pallas kernels for 0%

commit v1 on v0

v1 whole, which is shorter than its diff:
```python
import jax
import jax.numpy as jnp
from jax import lax
from jax.experimental import pallas as pl
from jax.experimental.pallas import tpu as pltpu
from jax.sharding import PartitionSpec as P

VARS = 8
LEV = 72
VL = VARS * LEV
LANES = 128
TAIL = 16
TOP = 32767.0
AXES = ("sec", "tile", "col")
VMEM = pl.BlockSpec(memory_space=pltpu.VMEM)
SMEM = pl.BlockSpec(memory_space=pltpu.SMEM)
INTERPRET = False


def roll(x, shift):
    return pltpu.roll(x, shift % LANES, x.ndim - 1)


def lane_index(rows):
    return lax.broadcasted_iota(jnp.int32, (rows, LANES), 1)


def encode_kernel(x_ref, msg_ref):
    rows = [x_ref[pl.ds(r, VL, stride=2), :] for r in range(2)]
    top = jnp.max(jnp.maximum(jnp.abs(rows[0]), jnp.abs(rows[1])), axis=0, keepdims=True)
    top = jnp.max(top, axis=1, keepdims=True)
    top = jnp.broadcast_to(jnp.maximum(top, 1e-30), (TAIL, LANES))
    code = jnp.ceil(jnp.log(top) * 64.0)
    scale = (TOP * jnp.exp(code * (-1.0 / 64.0)))[0:1, :]
    for r in range(2):
        q = jnp.clip(jnp.round(rows[r] * scale), -TOP, TOP)
        msg_ref[r * VL : (r + 1) * VL, :] = q.astype(jnp.int32).astype(jnp.int16)
    msg_ref[2 * VL :, :] = code.astype(jnp.int32).astype(jnp.int16)


def step_of(msg_ref):
    code = msg_ref[2 * VL :, :].astype(jnp.int32).astype(jnp.float32)
    return (jnp.exp(code * (1.0 / 64.0)) * (1.0 / TOP))[0:1, :]


def decode(msg_ref, r, step):
    return msg_ref[r * VL : (r + 1) * VL, :].astype(jnp.int32).astype(jnp.float32) * step


def edge_lanes(row, ri, packed, lane):
    for v in range(VARS):
        first = 16 * v + 4 * ri
        moved = roll(row[v * LEV : (v + 1) * LEV, :], first + 2)
        packed = jnp.where((lane >= first) & (lane < first + 4), moved, packed)
    return packed


def own_kernel(x_ref, diff_ref, edge_ref, surf_ref, spread_ref):
    lane = lane_index(LEV)
    packed = jnp.zeros((LEV, LANES), jnp.float32)
    for r in range(2):
        packed = edge_lanes(x_ref[pl.ds(r, VL, stride=2), :], r + 1, packed, lane)
        for v in range(VARS):
            surf_ref[r, v : v + 1, :] = x_ref[2 * LEV * v + r : 2 * LEV * v + r + 1, :]
    edge_ref[...] = packed
    diag = lax.broadcasted_iota(jnp.int32, (LANES, LANES), 0) == lax.broadcasted_iota(
        jnp.int32, (LANES, LANES), 1
    )
    for first in range(0, VL, LANES):
        size = min(LANES, VL - first)
        part = diff_ref[0:1, first : first + size]
        column = jnp.sum(jnp.where(diag[:size, :size], part, 0.0), axis=1, keepdims=True)
        spread_ref[first : first + size, :] = jnp.broadcast_to(column, (size, LANES))


def pack_kernel(up_ref, down_ref, edge_ref, surf_ref, full_ref, send_ref, table_ref):
    lane = lane_index(LEV)
    up_step, down_step = step_of(up_ref), step_of(down_ref)
    packed = edge_lanes(decode(up_ref, 1, up_step), 0, edge_ref[...], lane)
    packed = edge_lanes(decode(down_ref, 0, down_step), 3, packed, lane)
    full_ref[...] = packed
    send_ref[...] = packed.astype(jnp.bfloat16)
    for ref, step, base in ((up_ref, up_step, 0), (down_ref, down_step, 4)):
        for r in range(2):
            rows = []
            for v in range(VARS):
                at = r * VL + v * LEV
                block = ref[at // 16 * 16 : at // 16 * 16 + 16, :].astype(jnp.int32)
                rows.append(block[at % 16 : at % 16 + 1, :])
            block = jnp.concatenate(rows, axis=0).astype(jnp.float32) * step
            table_ref[base + r, :, :] = block.astype(jnp.bfloat16)
    for r in range(2):
        table_ref[2 + r, :, :] = surf_ref[r, :, :].astype(jnp.bfloat16)


def swap_inner(x, place):
    return jnp.where(place == 1, roll(x, -1), jnp.where(place == 2, roll(x, 1), x))


def first_kernel(x_ref, up_ref, down_ref, full_ref, recv_ref, spread_ref, op_ref, out_ref, rhs):
    up_step, down_step = step_of(up_ref), step_of(down_ref)
    lane = lane_index(LEV)
    place = lane % 4
    halo = recv_ref[...].astype(jnp.float32)
    own = full_ref[...]
    spread = jnp.zeros((LEV, LANES), jnp.float32)
    for v in range(VARS):
        spread = jnp.where(lane // 16 == v, spread_ref[v * LEV : (v + 1) * LEV, :], spread)
    beside = jnp.where(place == 1, roll(halo, 1) + roll(own, -1), roll(own, 1) + roll(halo, -1))
    corner = halo + spread * (roll(halo, 4) + roll(halo, -4) + beside - 4.0 * halo)
    corner = swap_inner(corner, place)
    halo = swap_inner(halo, place)

    for v in range(VARS):
        block = slice(v * LEV, (v + 1) * LEV)
        field = [
            decode_block(up_ref, 0, v, up_step),
            decode_block(up_ref, 1, v, up_step),
            x_ref[pl.ds(2 * LEV * v, LEV, stride=2), :],
            x_ref[pl.ds(2 * LEV * v + 1, LEV, stride=2), :],
            decode_block(down_ref, 0, v, down_step),
            decode_block(down_ref, 1, v, down_step),
        ]
        rate = spread_ref[block, :]
        for ri in range(4):
            center = field[ri + 1]
            ends = roll(halo, 126 - 16 * v - 4 * ri)
            left = jnp.where(lane == 0, ends, roll(center, 1))
            right = jnp.where(lane == LANES - 1, ends, roll(center, -1))
            center = center + rate * (field[ri + 2] + field[ri] + right + left - 4.0 * center)
            out_ref[ri, block, :] = center
            rhs[block, ri * LANES : (ri + 1) * LANES] = center.astype(jnp.bfloat16)
        moved = roll(corner, -16 * v)
        out_ref[4, block, :] = moved
        rhs[block, 4 * LANES :] = moved.astype(jnp.bfloat16)
    for ri in range(5):
        out_ref[ri] += jnp.dot(
            op_ref[0], rhs[:, ri * LANES : (ri + 1) * LANES], preferred_element_type=jnp.float32
        )


def decode_block(msg_ref, r, v, step):
    at = r * VL + v * LEV
    low = at // 16 * 16
    block = msg_ref[low : low + 80, :].astype(jnp.int32).astype(jnp.float32)
    return block[at - low : at - low + LEV, :] * step


def second_kernel(
    field_ref, spread_ref, op_ref, weight_ref, near_ref, far_ref, entry_ref, pick_ref, count_ref,
    out_ref, rhs,
):
    lane = lane_index(LEV)
    for v in range(VARS):
        block = slice(v * LEV, (v + 1) * LEV)
        rate = spread_ref[block, :]
        field = [field_ref[ri, block, :] for ri in range(5)]
        for r in range(2):
            ri = r + 1
            center = field[ri]
            ends = roll(field[4], 126 - 4 * ri)
            left = jnp.where(lane == 0, ends, roll(center, 1))
            right = jnp.where(lane == LANES - 1, ends, roll(center, -1))
            center = center + rate * (field[ri + 1] + field[ri - 1] + right + left - 4.0 * center)
            out_ref[pl.ds(2 * LEV * v + r, LEV, stride=2), :] = center
            rhs[block, r * LANES : (r + 1) * LANES] = center.astype(jnp.bfloat16)
    for r in range(2):
        out_ref[pl.ds(r, VL, stride=2), :] += jnp.dot(
            op_ref[0], rhs[:, r * LANES : (r + 1) * LANES], preferred_element_type=jnp.float32
        )
    mine = lax.axis_index("sec")
    last = lax.axis_size("sec") - 1
    for r in range(2):
        flux = jnp.zeros((VARS, LANES), jnp.float32)
        for slot in range(4):
            entry = entry_ref[0, r, 0, slot]
            source = jnp.where(mine == last, entry // 6, mine)
            within = entry % 6
            blocks = jnp.where(
                source == 0,
                near_ref[within],
                far_ref[jnp.where(source == 1, 6, 0) + within],
            )
            contrib = jnp.dot(
                blocks, weight_ref[pick_ref[0, r, 0, slot]], preferred_element_type=jnp.float32
            )
            flux = flux + jnp.where(slot < count_ref[0, r, 0], contrib, 0.0)
        flux = 0.5 * flux
        for v in range(VARS):
            at = 2 * LEV * v + r
            out_ref[at : at + 1, :] = out_ref[at : at + 1, :] + flux[v : v + 1, :]


def call(kernel, outs, specs, scratch=(), flops=0, moved=0):
    return pl.pallas_call(
        kernel,
        out_shape=[jax.ShapeDtypeStruct(shape, dtype) for shape, dtype in outs],
        in_specs=specs,
        out_specs=[VMEM] * len(outs),
        scratch_shapes=list(scratch),
        compiler_params=pltpu.CompilerParams(vmem_limit_bytes=40 * 2**20),
        cost_estimate=pl.CostEstimate(flops=flops, bytes_accessed=moved, transcendentals=0),
        interpret=INTERPRET,
    )


def solution(mesh):
    sections, tiles, cols = (mesh.shape[a] for a in AXES)

    def pairs(move):
        def index(s, t, c):
            return (s * tiles + t % tiles) * cols + c % cols

        return [
            (index(s, t, c), index(*move(s, t, c)))
            for s in range(sections)
            for t in range(tiles)
            for c in range(cols)
        ]

    def shards(state, column_op, diffusion, remap_weights, source_rows, weight_index, counts):
        x = state.reshape(2 * VL, LANES)
        (msg,) = call(encode_kernel, [((2 * VL + TAIL, LANES), jnp.int16)], [VMEM], moved=10**6)(x)
        up = lax.ppermute(msg, AXES, pairs(lambda s, t, c: (s, t + 1, c)))
        down = lax.ppermute(msg, AXES, pairs(lambda s, t, c: (s, t - 1, c)))
        edge, surf, spread = call(
            own_kernel,
            [((LEV, LANES), jnp.float32), ((2, VARS, LANES), jnp.float32), ((VL, LANES), jnp.float32)],
            [VMEM] * 2,
            moved=10**6,
        )(x, diffusion)
        full, send, table = call(
            pack_kernel,
            [((LEV, LANES), jnp.float32), ((LEV, LANES), jnp.bfloat16), ((6, VARS, LANES), jnp.bfloat16)],
            [VMEM] * 4,
            moved=10**6,
        )(up, down, edge, surf)
        near = lax.ppermute(table, AXES, pairs(lambda s, t, c: (3 - s, t, c)))
        recv = lax.ppermute(send, AXES, pairs(lambda s, t, c: (s, t, c + 1)))
        both = jnp.concatenate([table, near], axis=0)
        far = lax.ppermute(both, AXES, pairs(lambda s, t, c: (s ^ 1, t, c)))
        (field,) = call(
            first_kernel,
            [((5, VL, LANES), jnp.float32)],
            [VMEM] * 7,
            [pltpu.VMEM((VL, 5 * LANES), jnp.bfloat16)],
            flops=2 * VL * VL * 5 * LANES,
            moved=2 * 10**6,
        )(x, up, down, full, recv, spread, column_op)
        (out,) = call(
            second_kernel,
            [((2 * VL, LANES), jnp.float32)],
            [VMEM] * 6 + [SMEM] * 3,
            [pltpu.VMEM((VL, 2 * LANES), jnp.bfloat16)],
            flops=2 * VL * VL * 2 * LANES,
            moved=2 * 10**6,
        )(field, spread, column_op, remap_weights, near, far, source_rows, weight_index, counts)
        return out.reshape(1, VARS, LEV, 2, LANES)

    in_specs = (
        P("sec", None, None, "tile", "col"),
        P("sec", None, None),
        P("sec", None),
        P(),
        P("sec", "tile", "col", None),
        P("sec", "tile", "col", None),
        P("sec", "tile", "col"),
    )
    out_specs = P("sec", None, None, "tile", "col")
    return jax.shard_map(shards, mesh=mesh, in_specs=in_specs, out_specs=out_specs, check_vma=False)
```

time: 127 us -> 47.5 us (0.37); the launches traced: 125 us -> 47.2 us
  local copies, waits for them, and re-layouts: 37.5 us -> 1.87 us
  starting transfers between devices: 59.8 us -> 32.4 us
  blocking collectives: 13.1 us -> 0 us
  other arithmetic: 8.31 us -> 0.01 us
  waiting for transfers between devices: 1.36 us -> 7.92 us
  Pallas kernels: 0 us -> 4.8 us
  matrix products: 4.78 us -> 0 us
    ppermute x10 -> x5, starting transfers between devices: 59.8 us -> 32.4 us  [the longest x1 20.5 us: shards(): down = lax.ppermute(msg, AXES, pairs(lambda s, t, c: (s, t - 1, c)))]
    all_gather x1 -> x0, blocking collectives: 13.1 us -> none  [shards(): table = lax.all_gather(nearby, 'sec', axis=0, tiled=True)]
    gather x8 -> x0, local copies, waits for them, and re-layouts: 12.1 us -> none  [the longest x4 7.33 us: shards(): blocks = table[entries[:, slot_index]]]
    slice x8 -> x0, local copies, waits for them, and re-layouts: 9.37 us -> none  [the longest x4 7.28 us: with_halo(): head = lax.slice_in_dim(cells, 0, width, axis=dim)]
    ppermute x4 -> x0, local copies, waits for them, and re-layouts: 7.54 us -> none  [the longest x2 4.65 us: with_halo(): lax.ppermute(tail, axis, [(i, (i + 1) % count) for i in range(count)])]
    ppermute x10 -> x5, waiting for transfers between devices: 1.36 us -> 7.92 us  [the longest x1 4.66 us: shards(): recv = lax.ppermute(send, AXES, pairs(lambda s, t, c: (s, t, c + 1)))]
    convert_element_type x2 -> x0, other arithmetic: 5.43 us -> none  [physics(): field.astype(jnp.bfloat16)]
    pallas_call x0 -> x5, Pallas kernels: none -> 4.8 us  [the longest x1 2.37 us: shards(): call(second_kernel, [((2 * VL, LANES), jnp.float32)], [VMEM] * 6 + [SMEM]...]
  transfers between devices with their start and end apart: 10 -> 5, of which waited for: 1 -> 3; matrix products, arithmetic and copies ran while one was open for 17% -> 0% of each run, Pallas kernels for 0% -> 4%
where the time goes in v1:
time: 47.5 us; the launch traced here: 47.2 us
  starting transfers between devices  32.4 us (68%)
  waiting for transfers between devices  7.92 us (17%)
  Pallas kernels  4.8 us (10%)
  local copies, waits for them, and re-layouts  1.87 us (4%)
    ppermute x1, starting transfers between devices, shards(): down = lax.ppermute(msg, AXES, pairs(lambda s, t, c: (s, t - 1, c)))  20.5 us
    ppermute x1, starting transfers between devices, shards(): near = lax.ppermute(table, AXES, pairs(lambda s, t, c: (3 - s, t, c)))  5.08 us
    ppermute x1, waiting for transfers between devices, shards(): recv = lax.ppermute(send, AXES, pairs(lambda s, t, c: (s, t, c + 1)))  4.66 us
    ppermute x1, starting transfers between devices, shards(): far = lax.ppermute(both, AXES, pairs(lambda s, t, c: (s ^ 1, t, c)))  2.5 us
    pallas_call x1, Pallas kernels, shards(): call(second_kernel, [((2 * VL, LANES), jnp.float32)], [VMEM] * 6 + [SMEM]...  2.37 us
    ppermute x1, starting transfers between devices, shards(): recv = lax.ppermute(send, AXES, pairs(lambda s, t, c: (s, t, c + 1)))  2.35 us
    ppermute x1, starting transfers between devices, shards(): up = lax.ppermute(msg, AXES, pairs(lambda s, t, c: (s, t + 1, c)))  2.05 us
    unnamed x17, local copies, waits for them, and re-layouts  1.87 us
  transfers between devices with their start and end apart: 5, of which 3 were waited for; matrix products, arithmetic and copies ran while one was open for 0% of the time, Pallas kernels for 4%

profile of v1, /device:TPU:14, one launch (start us, length us, event | category | flops | bytes accessed | tf_op | source)
XLA Modules:
  0.0 47.2 jit_solution(2813361524926839211)
XLA Ops:
  0.0 0.0 copy-start.7
  0.0 0.0 copy-start
  0.0 1.1 %copy-done = f32[1,8,72,2,128]{4,3,2,1,0:T(2,128)S(1)} copy-done((f32[1,8,72,2,128]{4,3,2,1,0:T(2,128)S(1)}, f32[1,8,72,2,128]{4,3,2,1,0:T(2,128)}, u32[]{:S(2)}) %copy-start) | copy-done | bytes 589848
  1.1 0.0 copy-start.1
  1.1 0.0 copy-start.2
  1.1 0.2 shard_map.73
  1.3 2.1 %collective-permute-start = (s16[1168,128]{1,0:T(8,128)(2,1)S(1)}, s16[1168,128]{1,0:T(8,128)(2,1)S(1)}, u32[]{:S(2)}, u32[]{:S(2)}) collective-permute-start(s16[1168,128]{1,0:T(8,128)(2,1)S(1)} %shard_map.73), channel_id=1, source_target_pairs={{0,2},{1,3},{2,4},{3,5},{4,6},{5,7},{6,8},{7,9},{8,10},{9,11},{10,... | collective-permute-start | bytes 897032 | tf_op jit(solution)/shard_map/ppermute | solution.py:224
  3.4 20.5 %collective-permute-start.1 = (s16[1168,128]{1,0:T(8,128)(2,1)S(1)}, s16[1168,128]{1,0:T(8,128)(2,1)S(1)}, u32[]{:S(2)}, u32[]{:S(2)}) collective-permute-start(s16[1168,128]{1,0:T(8,128)(2,1)S(1)} %shard_map.73), channel_id=1, source_target_pairs={{0,254},{1,255},{2,0},{3,1},{4,2},{5,3},{6,4},{7,5},{8,6},{9,7},{1... | collective-permute-start | bytes 897032 | tf_op jit(solution)/shard_map/ppermute | solution.py:225
  23.9 0.0 copy-start.4
  23.9 0.7 %copy-done.4 = f32[1,576]{1,0:T(1,128)S(1)} copy-done((f32[1,576]{1,0:T(1,128)S(1)}, f32[1,576]{1,0:T(1,128)}, u32[]{:S(2)}) %copy-start.4) | copy-done | bytes 2328
  24.5 0.3 shard_map.74
  24.9 1.5 %collective-permute-done.up_ref = s16[1168,128]{1,0:T(8,128)(2,1)S(1)} collective-permute-done((s16[1168,128]{1,0:T(8,128)(2,1)S(1)}, s16[1168,128]{1,0:T(8,128)(2,1)S(1)}, u32[]{:S(2)}, u32[]{:S(2)}) %collective-permute-start) | collective-permute-done | bytes 299040 | tf_op jit(solution)/shard_map/ppermute | solution.py:224
  26.4 1.8 %collective-permute-done.1.down_ref = s16[1168,128]{1,0:T(8,128)(2,1)S(1)} collective-permute-done((s16[1168,128]{1,0:T(8,128)(2,1)S(1)}, s16[1168,128]{1,0:T(8,128)(2,1)S(1)}, u32[]{:S(2)}, u32[]{:S(2)}) %collective-permute-start.1) | collective-permute-done | bytes 299040 | tf_op jit(solution)/shard_map/ppermute | solution.py:225
  28.1 0.2 shard_map.75
  28.4 5.1 %collective-permute-start.3 = (bf16[6,8,128]{2,1,0:T(8,128)(2,1)S(1)}, bf16[6,8,128]{2,1,0:T(8,128)(2,1)S(1)}, u32[]{:S(2)}, u32[]{:S(2)}) collective-permute-start(bf16[6,8,128]{2,1,0:T(8,128)(2,1)S(1)} %get-tuple-element.16), channel_id=1, source_target_pairs={{0,768},{1,769},{2,770},{3,771},{4,772},{5,773},{6,774},{7,775},{8... | collective-permute-start | bytes 36872 | tf_op jit(solution)/shard_map/ppermute | solution.py:238
  33.4 0.0 copy-done.7
  33.5 0.1 copy.8.count_ref
  33.6 2.3 %collective-permute-start.2 = (bf16[72,128]{1,0:T(8,128)(2,1)S(1)}, bf16[72,128]{1,0:T(8,128)(2,1)S(1)}, u32[]{:S(2)}, u32[]{:S(2)}) collective-permute-start(bf16[72,128]{1,0:T(8,128)(2,1)S(1)} %get-tuple-element.14), channel_id=1, source_target_pairs={{0,1},{1,0},{2,3},{3,2},{4,5},{5,4},{6,7},{7,6},{8,9},{9,8},{10,11... | collective-permute-start | bytes 55304 | tf_op jit(solution)/shard_map/ppermute | solution.py:239
  35.9 0.0 collective-permute-done.3.near_ref
  35.9 2.5 %collective-permute-start.4 = (bf16[12,8,128]{2,1,0:T(8,128)(2,1)S(1)}, bf16[12,8,128]{2,1,0:T(8,128)(2,1)S(1)}, u32[]{:S(2)}, u32[]{:S(2)}) collective-permute-start(bf16[12,8,128]{2,1,0:T(8,128)(2,1)S(1)} %pad_maximum_fusion), channel_id=1, source_target_pairs={{0,256},{1,257},{2,258},{3,259},{4,260},{5,261},{6,262},{7,263},{8... | collective-permute-start | bytes 73736 | tf_op jit(solution)/shard_map/ppermute | solution.py:241
  38.4 4.7 %collective-permute-done.2.recv_ref = bf16[72,128]{1,0:T(8,128)(2,1)S(1)} collective-permute-done((bf16[72,128]{1,0:T(8,128)(2,1)S(1)}, bf16[72,128]{1,0:T(8,128)(2,1)S(1)}, u32[]{:S(2)}, u32[]{:S(2)}) %collective-permute-start.2) | collective-permute-done | bytes 18464 | tf_op jit(solution)/shard_map/ppermute | solution.py:239
  43.1 0.0 copy-done.1
  43.1 0.0 copy-done.2
  43.1 0.0 copy-start.3
  43.1 0.0 copy-start.5
  43.1 0.0 copy-start.6
  43.1 1.6 %shard_map.76.field_ref = f32[5,576,128]{2,1,0:T(8,128)S(1)} custom-call(f32[1152,128]{1,0:T(8,128)S(1)} %bitcast.4, s16[1168,128]{1,0:T(8,128)(2,1)S(1)} %collective-permute-done.up_ref, s16[1168,128]{1,0:T(8,128)(2,1)S(1)} %collective-permute-done.1.down_ref, f32[72,128]{1,0:T(8,128)S(1)} %get-tuple-element.13.full_ref, ...), custom_call_target="tpu_custom_call" | custom-call | flops 424673280 | bytes 2000000 | tf_op jit(solution)/shard_map/pallas_call | solution.py:242
  44.8 0.0 collective-permute-done.4.far_ref
  44.8 0.0 copy-done.3
  44.8 0.0 copy-done.5
  44.8 0.0 copy-done.6
  44.8 2.4 %shard_map.77 = f32[1152,128]{1,0:T(8,128)} custom-call(f32[5,576,128]{2,1,0:T(8,128)S(1)} %shard_map.76.field_ref, f32[576,128]{1,0:T(8,128)S(1)} %get-tuple-element.15.spread_ref, bf16[1,576,576]{2,1,0:T(8,128)(2,1)S(1)} %copy-done.2, bf16[32,128,128]{2,1,0:T(8,128)(2,1)S(1)} %copy-done.3, bf16[6,8,128]{2,1,0:T(8,128)(2,1)S(1)} %collective-permute-done.3.near_ref, ...), custom_call_target="tpu_custom_call" | custom-call | flops 169869312 | bytes 2000000 | tf_op jit(solution)/shard_map/pallas_call | solution.py:250
  (1 shorter events, 0.0 us)
Async XLA Ops:
  0.0 33.4 %copy-start.7 = (s32[1,2,1]{1,2,0:T(1,128)S(1)}, s32[1,2,1]{1,2,0:T(1,128)}, u32[]{:S(2)}) copy-start(s32[1,2,1]{1,2,0:T(1,128)} %param.13) | copy-start | bytes 28
  0.0 1.1 %copy-start = (f32[1,8,72,2,128]{4,3,2,1,0:T(2,128)S(1)}, f32[1,8,72,2,128]{4,3,2,1,0:T(2,128)}, u32[]{:S(2)}) copy-start(f32[1,8,72,2,128]{4,3,2,1,0:T(2,128)} %param.7) | copy-start | bytes 1769476
  1.1 42.0 %copy-start.1 = (f32[1,8,72,2,128]{4,3,2,1,0:T(2,128)S(1)}, f32[1,8,72,2,128]{4,3,2,1,0:T(2,128)}, u32[]{:S(2)}) copy-start(f32[1,8,72,2,128]{4,3,2,1,0:T(2,128)} %param.7) | copy-start | bytes 1769476
  1.1 42.0 %copy-start.2 = (bf16[1,576,576]{2,1,0:T(8,128)(2,1)S(1)}, bf16[1,576,576]{2,1,0:T(8,128)(2,1)}, u32[]{:S(2)}) copy-start(bf16[1,576,576]{2,1,0:T(8,128)(2,1)} %op_ref.3) | copy-start | bytes 1990660
  1.3 25.0 %collective-permute-start = (s16[1168,128]{1,0:T(8,128)(2,1)S(1)}, s16[1168,128]{1,0:T(8,128)(2,1)S(1)}, u32[]{:S(2)}, u32[]{:S(2)}) collective-permute-start(s16[1168,128]{1,0:T(8,128)(2,1)S(1)} %shard_map.73), channel_id=1, source_target_pairs={{0,2},{1,3},{2,4},{3,5},{4,6},{5,7},{6,8},{7,9},{8,10},{9,11},{10,... | collective-permute-start | bytes 897032 | tf_op jit(solution)/shard_map/ppermute | solution.py:224
  3.4 24.7 %collective-permute-start.1 = (s16[1168,128]{1,0:T(8,128)(2,1)S(1)}, s16[1168,128]{1,0:T(8,128)(2,1)S(1)}, u32[]{:S(2)}, u32[]{:S(2)}) collective-permute-start(s16[1168,128]{1,0:T(8,128)(2,1)S(1)} %shard_map.73), channel_id=1, source_target_pairs={{0,254},{1,255},{2,0},{3,1},{4,2},{5,3},{6,4},{7,5},{8,6},{9,7},{1... | collective-permute-start | bytes 897032 | tf_op jit(solution)/shard_map/ppermute | solution.py:225
  23.9 0.7 %copy-start.4 = (f32[1,576]{1,0:T(1,128)S(1)}, f32[1,576]{1,0:T(1,128)}, u32[]{:S(2)}) copy-start(f32[1,576]{1,0:T(1,128)} %diff_ref.1) | copy-start | bytes 6916
  28.4 7.6 %collective-permute-start.3 = (bf16[6,8,128]{2,1,0:T(8,128)(2,1)S(1)}, bf16[6,8,128]{2,1,0:T(8,128)(2,1)S(1)}, u32[]{:S(2)}, u32[]{:S(2)}) collective-permute-start(bf16[6,8,128]{2,1,0:T(8,128)(2,1)S(1)} %get-tuple-element.16), channel_id=1, source_target_pairs={{0,768},{1,769},{2,770},{3,771},{4,772},{5,773},{6,774},{7,775},{8... | collective-permute-start | bytes 36872 | tf_op jit(solution)/shard_map/ppermute | solution.py:238
  33.6 9.6 %collective-permute-start.2 = (bf16[72,128]{1,0:T(8,128)(2,1)S(1)}, bf16[72,128]{1,0:T(8,128)(2,1)S(1)}, u32[]{:S(2)}, u32[]{:S(2)}) collective-permute-start(bf16[72,128]{1,0:T(8,128)(2,1)S(1)} %get-tuple-element.14), channel_id=1, source_target_pairs={{0,1},{1,0},{2,3},{3,2},{4,5},{5,4},{6,7},{7,6},{8,9},{9,8},{10,11... | collective-permute-start | bytes 55304 | tf_op jit(solution)/shard_map/ppermute | solution.py:239
  35.9 8.8 %collective-permute-start.4 = (bf16[12,8,128]{2,1,0:T(8,128)(2,1)S(1)}, bf16[12,8,128]{2,1,0:T(8,128)(2,1)S(1)}, u32[]{:S(2)}, u32[]{:S(2)}) collective-permute-start(bf16[12,8,128]{2,1,0:T(8,128)(2,1)S(1)} %pad_maximum_fusion), channel_id=1, source_target_pairs={{0,256},{1,257},{2,258},{3,259},{4,260},{5,261},{6,262},{7,263},{8... | collective-permute-start | bytes 73736 | tf_op jit(solution)/shard_map/ppermute | solution.py:241
  43.1 1.7 %copy-start.3 = (bf16[32,128,128]{2,1,0:T(8,128)(2,1)S(1)}, bf16[32,128,128]{2,1,0:T(8,128)(2,1)}, u32[]{:S(2)}) copy-start(bf16[32,128,128]{2,1,0:T(8,128)(2,1)} %weight_ref.1) | copy-start | bytes 3145732
  43.1 1.7 %copy-start.5 = (s32[1,2,1,4]{3,2,1,0:T(1,128)S(1)}, s32[1,2,1,4]{3,2,1,0:T(1,128)}, u32[]{:S(2)}) copy-start(s32[1,2,1,4]{3,2,1,0:T(1,128)} %entry_ref.1) | copy-start | bytes 100
  43.1 1.7 %copy-start.6 = (s32[1,2,1,4]{3,2,1,0:T(1,128)S(1)}, s32[1,2,1,4]{3,2,1,0:T(1,128)}, u32[]{:S(2)}) copy-start(s32[1,2,1,4]{3,2,1,0:T(1,128)} %pick_ref.1) | copy-start | bytes 100

commit v2 on v1

v2 whole, which is shorter than its diff:
```python
import jax
import jax.numpy as jnp
from jax import lax
from jax.experimental import pallas as pl
from jax.experimental.pallas import tpu as pltpu
from jax.sharding import PartitionSpec as P

VARS = 8
LEV = 72
VL = VARS * LEV
LANES = 128
TAIL = 16
TOP = 32767.0
AXES = ("sec", "tile", "col")
VMEM = pl.BlockSpec(memory_space=pltpu.VMEM)
HBM = pl.BlockSpec(memory_space=pltpu.HBM)
SMEM = pl.BlockSpec(memory_space=pltpu.SMEM)


def roll(x, shift):
    return pltpu.roll(x, shift % LANES, x.ndim - 1)


def lane_index(rows):
    return lax.broadcasted_iota(jnp.int32, (rows, LANES), 1)


def side():
    return lax.axis_index("tile") % 2


def encode_kernel(x_ref, msg_ref):
    top = jnp.max(jnp.abs(x_ref[...]), axis=0, keepdims=True)
    top = jnp.max(top, axis=1, keepdims=True)
    rows = [x_ref[pl.ds(side(), VL, stride=2), :], x_ref[pl.ds(1 - side(), VL, stride=2), :]]
    top = jnp.broadcast_to(jnp.maximum(top, 1e-30), (TAIL, LANES))
    code = jnp.ceil(jnp.log(top) * 64.0)
    scale = (TOP * jnp.exp(code * (-1.0 / 64.0)))[0:1, :]
    for r in range(2):
        q = jnp.clip(jnp.round(rows[r] * scale), -TOP, TOP)
        msg_ref[r * VL : (r + 1) * VL, :] = q.astype(jnp.int32).astype(jnp.int16)
    msg_ref[2 * VL :, :] = code.astype(jnp.int32).astype(jnp.int16)


def step_of(msg_ref):
    code = msg_ref[2 * VL :, :].astype(jnp.int32).astype(jnp.float32)
    return (jnp.exp(code * (1.0 / 64.0)) * (1.0 / TOP))[0:1, :]


def decode(msg_ref, r, step):
    return msg_ref[r * VL : (r + 1) * VL, :].astype(jnp.int32).astype(jnp.float32) * step


def edge_lanes(row, ri, packed, lane):
    for v in range(VARS):
        first = 16 * v + 4 * ri
        moved = roll(row[v * LEV : (v + 1) * LEV, :], first + 2)
        packed = jnp.where((lane >= first) & (lane < first + 4), moved, packed)
    return packed


def own_kernel(x_ref, diff_ref, edge_ref, surf_ref, spread_ref):
    lane = lane_index(LEV)
    packed = jnp.zeros((LEV, LANES), jnp.float32)
    for r in range(2):
        place = side() if r == 0 else 1 - side()
        packed = edge_lanes(x_ref[pl.ds(place, VL, stride=2), :], r + 1, packed, lane)
        for v in range(VARS):
            surf_ref[r, v : v + 1, :] = x_ref[pl.ds(2 * LEV * v + place, 1), :]
    edge_ref[...] = packed
    diag = lax.broadcasted_iota(jnp.int32, (LANES, LANES), 0) == lax.broadcasted_iota(
        jnp.int32, (LANES, LANES), 1
    )
    for first in range(0, VL, LANES):
        size = min(LANES, VL - first)
        part = diff_ref[0:1, first : first + size]
        column = jnp.sum(jnp.where(diag[:size, :size], part, 0.0), axis=1, keepdims=True)
        spread_ref[first : first + size, :] = jnp.broadcast_to(column, (size, LANES))


def pack_kernel(link_ref, mate_ref, edge_ref, surf_ref, full_ref, send_ref, table_ref):
    lane = lane_index(LEV)
    link_step, mate_step = step_of(link_ref), step_of(mate_ref)
    packed = edge_lanes(decode(link_ref, 0, link_step), 0, edge_ref[...], lane)
    packed = edge_lanes(decode(mate_ref, 1, mate_step), 3, packed, lane)
    full_ref[...] = packed
    send_ref[...] = packed.astype(jnp.bfloat16)
    for r in range(2):
        rows, others = [], []
        for v in range(VARS):
            at = (1 - r) * VL + v * LEV
            low = at // 16 * 16
            block = link_ref[low : low + 16, :].astype(jnp.int32)
            rows.append(block[at - low : at - low + 1, :].astype(jnp.float32) * link_step)
            block = mate_ref[low : low + 16, :].astype(jnp.int32)
            others.append(block[at - low : at - low + 1, :].astype(jnp.float32) * mate_step)
        table_ref[r, :, :] = jnp.concatenate(rows, axis=0).astype(jnp.bfloat16)
        table_ref[2 + r, :, :] = surf_ref[r, :, :].astype(jnp.bfloat16)
        table_ref[4 + r, :, :] = jnp.concatenate(others, axis=0).astype(jnp.bfloat16)


def swap_inner(x, place):
    return jnp.where(place == 1, roll(x, -1), jnp.where(place == 2, roll(x, 1), x))


def first_substep(
    x_ref, link_ref, mate_ref, full_ref, halo, spread_ref, op_ref, out_ref, rhs
):
    link_step, mate_step = step_of(link_ref), step_of(mate_ref)
    lane = lane_index(LEV)
    place = lane % 4
    own = full_ref[...]
    spread = jnp.zeros((LEV, LANES), jnp.float32)
    for v in range(VARS):
        spread = jnp.where(lane // 16 == v, spread_ref[v * LEV : (v + 1) * LEV, :], spread)
    beside = jnp.where(place == 1, roll(halo, 1) + roll(own, -1), roll(own, 1) + roll(halo, -1))
    corner = halo + spread * (roll(halo, 4) + roll(halo, -4) + beside - 4.0 * halo)
    corner = swap_inner(corner, place)
    halo = swap_inner(halo, place)

    for v in range(VARS):
        block = slice(v * LEV, (v + 1) * LEV)
        field = [
            decode_block(link_ref, 1, v, link_step),
            decode_block(link_ref, 0, v, link_step),
            x_ref[pl.ds(2 * LEV * v + side(), LEV, stride=2), :],
            x_ref[pl.ds(2 * LEV * v + 1 - side(), LEV, stride=2), :],
            decode_block(mate_ref, 1, v, mate_step),
            decode_block(mate_ref, 0, v, mate_step),
        ]
        rate = spread_ref[block, :]
        for ri in range(4):
            center = field[ri + 1]
            ends = roll(halo, 126 - 16 * v - 4 * ri)
            left = jnp.where(lane == 0, ends, roll(center, 1))
            right = jnp.where(lane == LANES - 1, ends, roll(center, -1))
            center = center + rate * (field[ri + 2] + field[ri] + right + left - 4.0 * center)
            out_ref[ri, block, :] = center
            rhs[block, ri * LANES : (ri + 1) * LANES] = center.astype(jnp.bfloat16)
        moved = roll(corner, -16 * v)
        out_ref[4, block, :] = moved
        rhs[block, 4 * LANES :] = moved.astype(jnp.bfloat16)
    for ri in range(0, 5, 2):
        width = min(2, 5 - ri)
        tendency = jnp.dot(
            op_ref[0],
            rhs[:, ri * LANES : (ri + width) * LANES],
            preferred_element_type=jnp.float32,
        )
        for k in range(width):
            out_ref[ri + k] += tendency[:, k * LANES : (k + 1) * LANES]


def decode_block(msg_ref, r, v, step):
    at = r * VL + v * LEV
    low = at // 16 * 16
    block = msg_ref[low : low + 80, :].astype(jnp.int32).astype(jnp.float32)
    return block[at - low : at - low + LEV, :] * step


def second_substep(field_ref, spread_ref, op_ref, out_ref, rhs, fluxes, out_hbm, sems):
    lane = lane_index(LEV)
    place = side()
    for v in range(VARS):
        block = slice(v * LEV, (v + 1) * LEV)
        rate = spread_ref[block, :]
        field = [field_ref[ri, block, :] for ri in range(5)]
        for r in range(2):
            ri = r + 1
            center = field[ri]
            ends = roll(field[4], 126 - 4 * ri)
            left = jnp.where(lane == 0, ends, roll(center, 1))
            right = jnp.where(lane == LANES - 1, ends, roll(center, -1))
            center = center + rate * (field[ri + 1] + field[ri - 1] + right + left - 4.0 * center)
            at = 2 * LEV * v + (place if r == 0 else 1 - place)
            out_ref[pl.ds(at, LEV, stride=2), :] = center
            rhs[block, r * LANES : (r + 1) * LANES] = center.astype(jnp.bfloat16)
    half = VL // 2
    copies = []
    for part in range(2):
        tendency = jnp.dot(
            op_ref[0, part * half : (part + 1) * half, :],
            rhs[:, : 2 * LANES],
            preferred_element_type=jnp.float32,
        )
        for r in range(2):
            rows = pl.ds(2 * half * part + (place if r == 0 else 1 - place), half, stride=2)
            out_ref[rows, :] += tendency[:, r * LANES : (r + 1) * LANES]
        for v in range(part * VARS // 2, (part + 1) * VARS // 2):
            for r in range(2):
                at = 2 * LEV * v + r
                out_ref[at : at + 1, :] = out_ref[at : at + 1, :] + fluxes[r][v : v + 1, :]
        rows = pl.ds(part * VL, VL)
        copies.append(pltpu.make_async_copy(out_ref.at[rows, :], out_hbm.at[rows, :], sems.at[part]))
        copies[part].start()
    for copy in copies:
        copy.wait()


def flux_of(weight_ref, near_ref, far_ref, entry_ref, pick_ref, count_ref):
    mine = lax.axis_index("sec")
    place = side()
    fluxes = []
    for r in range(2):
        blocks, weights = [], []
        for slot in range(4):
            entry = entry_ref[0, r, 0, slot]
            apart = mine ^ (entry // 6)
            within = entry % 6
            within = jnp.where(place == 0, within, 5 - within)
            block = jnp.where(
                apart == 2, near_ref[within], far_ref[jnp.where(apart == 3, 6, 0) + within]
            )
            blocks.append(jnp.where(slot < count_ref[0, r, 0], block, jnp.zeros_like(block)))
            weights.append(weight_ref[pick_ref[0, r, 0, slot]])
        fluxes.append(
            0.5
            * jnp.dot(
                jnp.concatenate(blocks, axis=1),
                jnp.concatenate(weights, axis=0),
                preferred_element_type=jnp.float32,
            )
        )
    return fluxes


def first_kernel(
    x_ref, link_ref, mate_ref, full_ref, recv_ref, spread_ref, op_ref, near_rows, rhs
):
    halo = recv_ref[...].astype(jnp.float32)
    first_substep(x_ref, link_ref, mate_ref, full_ref, halo, spread_ref, op_ref, near_rows, rhs)


def second_kernel(
    near_rows, spread_ref, op_ref, weight_ref, near_ref, far_ref, entry_ref, pick_ref, count_ref,
    out_hbm, rhs, out_ref, sems,
):
    fluxes = flux_of(weight_ref, near_ref, far_ref, entry_ref, pick_ref, count_ref)
    second_substep(near_rows, spread_ref, op_ref, out_ref, rhs, fluxes, out_hbm, sems)


def call(kernel, outs, specs, scratch=(), flops=0, moved=0, out_specs=None):
    return pl.pallas_call(
        kernel,
        out_shape=[jax.ShapeDtypeStruct(shape, dtype) for shape, dtype in outs],
        in_specs=specs,
        out_specs=out_specs or [VMEM] * len(outs),
        scratch_shapes=list(scratch),
        compiler_params=pltpu.CompilerParams(vmem_limit_bytes=40 * 2**20),
        cost_estimate=pl.CostEstimate(flops=flops, bytes_accessed=moved, transcendentals=0),
    )


def solution(mesh):
    sections, tiles, cols = (mesh.shape[a] for a in AXES)

    def send(x, move):
        def index(s, t, c):
            return (s * tiles + t) * cols + c

        pairs = [
            (index(s, t, c), index(*move(s, t, c)))
            for s in range(sections)
            for t in range(tiles)
            for c in range(cols)
        ]
        return lax.ppermute(x, AXES, pairs)

    def shards(state, column_op, diffusion, remap_weights, source_rows, weight_index, counts):
        x = state.reshape(2 * VL, LANES)
        wide, narrow = ((LEV, LANES), jnp.float32), ((LEV, LANES), jnp.bfloat16)
        (msg,) = call(encode_kernel, [((2 * VL + TAIL, LANES), jnp.int16)], [VMEM], moved=10**6)(x)
        link = send(msg, lambda s, t, c: (s, (t - 1 + 2 * (t % 2)) % tiles, c))
        mate = send(msg, lambda s, t, c: (s, t + 1 - 2 * (t % 2), c))
        edge, surf, spread = call(
            own_kernel,
            [wide, ((2, VARS, LANES), jnp.float32), ((VL, LANES), jnp.float32)],
            [VMEM] * 2,
            moved=10**6,
        )(x, diffusion)
        full, full16, table = call(
            pack_kernel,
            [wide, narrow, ((6, VARS, LANES), jnp.bfloat16)],
            [VMEM] * 4,
            moved=10**6,
        )(link, mate, edge, surf)
        near = send(table, lambda s, t, c: (s ^ 2, t, c))
        recv = send(full16, lambda s, t, c: (s, t, 1 - c))
        both = jnp.concatenate([table, near], axis=0)
        far = send(both, lambda s, t, c: (s ^ 1, t, c))
        (rows,) = call(
            first_kernel,
            [((5, VL, LANES), jnp.float32)],
            [VMEM] * 7,
            [pltpu.VMEM((VL, 5 * LANES), jnp.bfloat16)],
            flops=2 * VL * VL * 5 * LANES,
            moved=2 * 10**6,
        )(x, link, mate, full, recv, spread, column_op)
        (out,) = call(
            second_kernel,
            [((2 * VL, LANES), jnp.float32)],
            [VMEM] * 6 + [SMEM] * 3,
            [
                pltpu.VMEM((VL, 2 * LANES), jnp.bfloat16),
                pltpu.VMEM((2 * VL, LANES), jnp.float32),
                pltpu.SemaphoreType.DMA((2,)),
            ],
            flops=2 * VL * VL * 2 * LANES,
            moved=2 * 10**6,
            out_specs=[HBM],
        )(rows, spread, column_op, remap_weights, near, far, source_rows, weight_index, counts)
        return out.reshape(1, VARS, LEV, 2, LANES)

    in_specs = (
        P("sec", None, None, "tile", "col"),
        P("sec", None, None),
        P("sec", None),
        P(),
        P("sec", "tile", "col", None),
        P("sec", "tile", "col", None),
        P("sec", "tile", "col"),
    )
    out_specs = P("sec", None, None, "tile", "col")
    return jax.shard_map(shards, mesh=mesh, in_specs=in_specs, out_specs=out_specs, check_vma=False)
```

time: 47.5 us -> 45.2 us (0.952)
  waiting for transfers between devices: 7.92 us -> 5.33 us
    ppermute x5, waiting for transfers between devices: 7.92 us -> 5.33 us  [send(): return lax.ppermute(x, AXES, pairs)]
  transfers between devices with their start and end apart: 5 -> 5, of which waited for: 3 -> 2; matrix products, arithmetic and copies ran while one was open for 0% -> 0% of each run, Pallas kernels for 4% -> 4%
where the time goes in v2:
time: 45.2 us; the launch traced here: 44.4 us
  starting transfers between devices  32.4 us (72%)
  waiting for transfers between devices  5.33 us (12%)
  Pallas kernels  4.67 us (10%)
  local copies, waits for them, and re-layouts  1.87 us (4%)
    ppermute x5, starting transfers between devices, send(): return lax.ppermute(x, AXES, pairs)  32.4 us
    ppermute x5, waiting for transfers between devices, send(): return lax.ppermute(x, AXES, pairs)  5.33 us
    pallas_call x1, Pallas kernels, shards(): call(second_kernel, [((2 * VL, LANES), jnp.float32)], [VMEM] * 6 + [SMEM]...  2.28 us
    unnamed x17, local copies, waits for them, and re-layouts  1.87 us
    pallas_call x1, Pallas kernels, shards(): call(first_kernel, [((5, VL, LANES), jnp.float32)], [VMEM] * 7, [pltpu.VM...  1.59 us
  transfers between devices with their start and end apart: 5, of which 2 were waited for; matrix products, arithmetic and copies ran while one was open for 0% of the time, Pallas kernels for 4%

profile of v2, /device:TPU:14, one launch (start us, length us, event | category | flops | bytes accessed | tf_op | source)
XLA Modules:
  0.0 44.4 jit_solution(8847413042439651550)
XLA Ops:
  0.0 0.0 copy-start.7
  0.0 0.0 copy-start
  0.0 1.1 %copy-done = f32[1,8,72,2,128]{4,3,2,1,0:T(2,128)S(1)} copy-done((f32[1,8,72,2,128]{4,3,2,1,0:T(2,128)S(1)}, f32[1,8,72,2,128]{4,3,2,1,0:T(2,128)}, u32[]{:S(2)}) %copy-start) | copy-done | bytes 589848
  1.1 0.0 copy-start.1
  1.1 0.0 copy-start.2
  1.1 0.2 shard_map.73
  1.3 20.6 %collective-permute-start = (s16[1168,128]{1,0:T(8,128)(2,1)S(1)}, s16[1168,128]{1,0:T(8,128)(2,1)S(1)}, u32[]{:S(2)}, u32[]{:S(2)}) collective-permute-start(s16[1168,128]{1,0:T(8,128)(2,1)S(1)} %shard_map.73), channel_id=1, source_target_pairs={{0,254},{1,255},{2,4},{3,5},{4,2},{5,3},{6,8},{7,9},{8,6},{9,7},{1... | collective-permute-start | bytes 897032 | tf_op jit(solution)/shard_map/ppermute | solution.py:267
  21.9 1.9 %collective-permute-start.1 = (s16[1168,128]{1,0:T(8,128)(2,1)S(1)}, s16[1168,128]{1,0:T(8,128)(2,1)S(1)}, u32[]{:S(2)}, u32[]{:S(2)}) collective-permute-start(s16[1168,128]{1,0:T(8,128)(2,1)S(1)} %shard_map.73), channel_id=1, source_target_pairs={{0,2},{1,3},{2,0},{3,1},{4,6},{5,7},{6,4},{7,5},{8,10},{9,11},{10,... | collective-permute-start | bytes 897032 | tf_op jit(solution)/shard_map/ppermute | solution.py:267
  23.9 0.0 copy-start.4
  23.9 0.7 %copy-done.4 = f32[1,576]{1,0:T(1,128)S(1)} copy-done((f32[1,576]{1,0:T(1,128)S(1)}, f32[1,576]{1,0:T(1,128)}, u32[]{:S(2)}) %copy-start.4) | copy-done | bytes 2328
  24.5 0.3 shard_map.74
  24.9 1.5 %collective-permute-done.link_ref = s16[1168,128]{1,0:T(8,128)(2,1)S(1)} collective-permute-done((s16[1168,128]{1,0:T(8,128)(2,1)S(1)}, s16[1168,128]{1,0:T(8,128)(2,1)S(1)}, u32[]{:S(2)}, u32[]{:S(2)}) %collective-permute-start) | collective-permute-done | bytes 299040 | tf_op jit(solution)/shard_map/ppermute | solution.py:267
  26.4 0.0 collective-permute-done.1.mate_ref
  26.4 0.2 shard_map.75
  26.6 4.2 %collective-permute-start.3 = (bf16[6,8,128]{2,1,0:T(8,128)(2,1)S(1)}, bf16[6,8,128]{2,1,0:T(8,128)(2,1)S(1)}, u32[]{:S(2)}, u32[]{:S(2)}) collective-permute-start(bf16[6,8,128]{2,1,0:T(8,128)(2,1)S(1)} %get-tuple-element.16), channel_id=1, source_target_pairs={{0,512},{1,513},{2,514},{3,515},{4,516},{5,517},{6,518},{7,519},{8... | collective-permute-start | bytes 36872 | tf_op jit(solution)/shard_map/ppermute | solution.py:267
  30.8 0.0 copy-done.7
  30.8 0.1 copy.8.count_ref
  30.9 3.2 %collective-permute-start.2 = (bf16[72,128]{1,0:T(8,128)(2,1)S(1)}, bf16[72,128]{1,0:T(8,128)(2,1)S(1)}, u32[]{:S(2)}, u32[]{:S(2)}) collective-permute-start(bf16[72,128]{1,0:T(8,128)(2,1)S(1)} %get-tuple-element.14), channel_id=1, source_target_pairs={{0,1},{1,0},{2,3},{3,2},{4,5},{5,4},{6,7},{7,6},{8,9},{9,8},{10,11... | collective-permute-start | bytes 55304 | tf_op jit(solution)/shard_map/ppermute | solution.py:267
  34.2 0.0 collective-permute-done.3.near_ref
  34.2 2.4 %collective-permute-start.4 = (bf16[12,8,128]{2,1,0:T(8,128)(2,1)S(1)}, bf16[12,8,128]{2,1,0:T(8,128)(2,1)S(1)}, u32[]{:S(2)}, u32[]{:S(2)}) collective-permute-start(bf16[12,8,128]{2,1,0:T(8,128)(2,1)S(1)} %pad_maximum_fusion), channel_id=1, source_target_pairs={{0,256},{1,257},{2,258},{3,259},{4,260},{5,261},{6,262},{7,263},{8... | collective-permute-start | bytes 73736 | tf_op jit(solution)/shard_map/ppermute | solution.py:267
  36.7 3.8 %collective-permute-done.2.recv_ref = bf16[72,128]{1,0:T(8,128)(2,1)S(1)} collective-permute-done((bf16[72,128]{1,0:T(8,128)(2,1)S(1)}, bf16[72,128]{1,0:T(8,128)(2,1)S(1)}, u32[]{:S(2)}, u32[]{:S(2)}) %collective-permute-start.2) | collective-permute-done | bytes 18464 | tf_op jit(solution)/shard_map/ppermute | solution.py:267
  40.5 0.0 copy-done.1
  40.5 0.0 copy-done.2
  40.5 0.0 copy-start.3
  40.5 0.0 copy-start.5
  40.5 0.0 copy-start.6
  40.5 1.6 %shard_map.76.near_rows = f32[5,576,128]{2,1,0:T(8,128)S(1)} custom-call(f32[1152,128]{1,0:T(8,128)S(1)} %bitcast.4, s16[1168,128]{1,0:T(8,128)(2,1)S(1)} %collective-permute-done.link_ref, s16[1168,128]{1,0:T(8,128)(2,1)S(1)} %collective-permute-done.1.mate_ref, f32[72,128]{1,0:T(8,128)S(1)} %get-tuple-element.13.full_ref, ...), custom_call_target="tpu_custom_call" | custom-call | flops 424673280 | bytes 2000000 | tf_op jit(solution)/shard_map/pallas_call | solution.py:291
  42.1 0.0 collective-permute-done.4.far_ref
  42.1 0.0 copy-done.3
  42.1 0.0 copy-done.5
  42.1 0.0 copy-done.6
  42.2 2.3 %shard_map.77 = f32[1152,128]{1,0:T(8,128)} custom-call(f32[5,576,128]{2,1,0:T(8,128)S(1)} %shard_map.76.near_rows, f32[576,128]{1,0:T(8,128)S(1)} %get-tuple-element.15.spread_ref, bf16[1,576,576]{2,1,0:T(8,128)(2,1)S(1)} %copy-done.2, bf16[32,128,128]{2,1,0:T(8,128)(2,1)S(1)} %copy-done.3, bf16[6,8,128]{2,1,0:T(8,128)(2,1)S(1)} %collective-permute-done.3.near_ref, ...), custom_call_target="tpu_custom_call" | custom-call | flops 169869312 | bytes 2000000 | tf_op jit(solution)/shard_map/pallas_call | solution.py:299
  (1 shorter events, 0.0 us)
Async XLA Ops:
  0.0 30.8 %copy-start.7 = (s32[1,2,1]{1,2,0:T(1,128)S(1)}, s32[1,2,1]{1,2,0:T(1,128)}, u32[]{:S(2)}) copy-start(s32[1,2,1]{1,2,0:T(1,128)} %param.13) | copy-start | bytes 28
  0.0 1.1 %copy-start = (f32[1,8,72,2,128]{4,3,2,1,0:T(2,128)S(1)}, f32[1,8,72,2,128]{4,3,2,1,0:T(2,128)}, u32[]{:S(2)}) copy-start(f32[1,8,72,2,128]{4,3,2,1,0:T(2,128)} %param.7) | copy-start | bytes 1769476
  1.1 39.4 %copy-start.1 = (f32[1,8,72,2,128]{4,3,2,1,0:T(2,128)S(1)}, f32[1,8,72,2,128]{4,3,2,1,0:T(2,128)}, u32[]{:S(2)}) copy-start(f32[1,8,72,2,128]{4,3,2,1,0:T(2,128)} %param.7) | copy-start | bytes 1769476
  1.1 39.4 %copy-start.2 = (bf16[1,576,576]{2,1,0:T(8,128)(2,1)S(1)}, bf16[1,576,576]{2,1,0:T(8,128)(2,1)}, u32[]{:S(2)}) copy-start(bf16[1,576,576]{2,1,0:T(8,128)(2,1)} %op_ref.3) | copy-start | bytes 1990660
  1.3 25.0 %collective-permute-start = (s16[1168,128]{1,0:T(8,128)(2,1)S(1)}, s16[1168,128]{1,0:T(8,128)(2,1)S(1)}, u32[]{:S(2)}, u32[]{:S(2)}) collective-permute-start(s16[1168,128]{1,0:T(8,128)(2,1)S(1)} %shard_map.73), channel_id=1, source_target_pairs={{0,254},{1,255},{2,4},{3,5},{4,2},{5,3},{6,8},{7,9},{8,6},{9,7},{1... | collective-permute-start | bytes 897032 | tf_op jit(solution)/shard_map/ppermute | solution.py:267
  21.9 4.4 %collective-permute-start.1 = (s16[1168,128]{1,0:T(8,128)(2,1)S(1)}, s16[1168,128]{1,0:T(8,128)(2,1)S(1)}, u32[]{:S(2)}, u32[]{:S(2)}) collective-permute-start(s16[1168,128]{1,0:T(8,128)(2,1)S(1)} %shard_map.73), channel_id=1, source_target_pairs={{0,2},{1,3},{2,0},{3,1},{4,6},{5,7},{6,4},{7,5},{8,10},{9,11},{10,... | collective-permute-start | bytes 897032 | tf_op jit(solution)/shard_map/ppermute | solution.py:267
  23.9 0.7 %copy-start.4 = (f32[1,576]{1,0:T(1,128)S(1)}, f32[1,576]{1,0:T(1,128)}, u32[]{:S(2)}) copy-start(f32[1,576]{1,0:T(1,128)} %diff_ref.1) | copy-start | bytes 6916
  26.6 7.6 %collective-permute-start.3 = (bf16[6,8,128]{2,1,0:T(8,128)(2,1)S(1)}, bf16[6,8,128]{2,1,0:T(8,128)(2,1)S(1)}, u32[]{:S(2)}, u32[]{:S(2)}) collective-permute-start(bf16[6,8,128]{2,1,0:T(8,128)(2,1)S(1)} %get-tuple-element.16), channel_id=1, source_target_pairs={{0,512},{1,513},{2,514},{3,515},{4,516},{5,517},{6,518},{7,519},{8... | collective-permute-start | bytes 36872 | tf_op jit(solution)/shard_map/ppermute | solution.py:267
  30.9 9.6 %collective-permute-start.2 = (bf16[72,128]{1,0:T(8,128)(2,1)S(1)}, bf16[72,128]{1,0:T(8,128)(2,1)S(1)}, u32[]{:S(2)}, u32[]{:S(2)}) collective-permute-start(bf16[72,128]{1,0:T(8,128)(2,1)S(1)} %get-tuple-element.14), channel_id=1, source_target_pairs={{0,1},{1,0},{2,3},{3,2},{4,5},{5,4},{6,7},{7,6},{8,9},{9,8},{10,11... | collective-permute-start | bytes 55304 | tf_op jit(solution)/shard_map/ppermute | solution.py:267
  34.2 7.9 %collective-permute-start.4 = (bf16[12,8,128]{2,1,0:T(8,128)(2,1)S(1)}, bf16[12,8,128]{2,1,0:T(8,128)(2,1)S(1)}, u32[]{:S(2)}, u32[]{:S(2)}) collective-permute-start(bf16[12,8,128]{2,1,0:T(8,128)(2,1)S(1)} %pad_maximum_fusion), channel_id=1, source_target_pairs={{0,256},{1,257},{2,258},{3,259},{4,260},{5,261},{6,262},{7,263},{8... | collective-permute-start | bytes 73736 | tf_op jit(solution)/shard_map/ppermute | solution.py:267
  40.5 1.6 %copy-start.3 = (bf16[32,128,128]{2,1,0:T(8,128)(2,1)S(1)}, bf16[32,128,128]{2,1,0:T(8,128)(2,1)}, u32[]{:S(2)}) copy-start(bf16[32,128,128]{2,1,0:T(8,128)(2,1)} %weight_ref.1) | copy-start | bytes 3145732
  40.5 1.6 %copy-start.5 = (s32[1,2,1,4]{3,2,1,0:T(1,128)S(1)}, s32[1,2,1,4]{3,2,1,0:T(1,128)}, u32[]{:S(2)}) copy-start(s32[1,2,1,4]{3,2,1,0:T(1,128)} %entry_ref.1) | copy-start | bytes 100
  40.5 1.6 %copy-start.6 = (s32[1,2,1,4]{3,2,1,0:T(1,128)S(1)}, s32[1,2,1,4]{3,2,1,0:T(1,128)}, u32[]{:S(2)}) copy-start(s32[1,2,1,4]{3,2,1,0:T(1,128)} %pick_ref.1) | copy-start | bytes 100

commit v3 on v2

--- a/solution.py
+++ b/solution.py
@@ -10,6 +10,7 @@
 VL = VARS * LEV
 LANES = 128
 TAIL = 16
+FOLD = 16
 TOP = 32767.0
 AXES = ("sec", "tile", "col")
 VMEM = pl.BlockSpec(memory_space=pltpu.VMEM)
@@ -29,7 +30,7 @@
     return lax.axis_index("tile") % 2
 
 
-def encode_kernel(x_ref, msg_ref):
+def encode_kernel(x_ref, link_ref, mate_ref):
     top = jnp.max(jnp.abs(x_ref[...]), axis=0, keepdims=True)
     top = jnp.max(top, axis=1, keepdims=True)
     rows = [x_ref[pl.ds(side(), VL, stride=2), :], x_ref[pl.ds(1 - side(), VL, stride=2), :]]
@@ -38,12 +39,17 @@
     scale = (TOP * jnp.exp(code * (-1.0 / 64.0)))[0:1, :]
     for r in range(2):
         q = jnp.clip(jnp.round(rows[r] * scale), -TOP, TOP)
-        msg_ref[r * VL : (r + 1) * VL, :] = q.astype(jnp.int32).astype(jnp.int16)
-    msg_ref[2 * VL :, :] = code.astype(jnp.int32).astype(jnp.int16)
+        q = q.astype(jnp.int32).astype(jnp.int16)
+        link_ref[r * VL : (r + 1) * VL, :] = q
+        mate_ref[r * VL : (r + 1) * VL, :] = q
+    code = code.astype(jnp.int32).astype(jnp.int16)
+    mate_ref[2 * VL :, :] = code
+    link_ref[2 * VL : 2 * VL + TAIL, :] = code
+    link_ref[2 * VL + TAIL :, :] = code
 
 
 def step_of(msg_ref):
-    code = msg_ref[2 * VL :, :].astype(jnp.int32).astype(jnp.float32)
+    code = msg_ref[2 * VL : 2 * VL + TAIL, :].astype(jnp.int32).astype(jnp.float32)
     return (jnp.exp(code * (1.0 / 64.0)) * (1.0 / TOP))[0:1, :]
 
 
@@ -57,6 +63,36 @@
         moved = roll(row[v * LEV : (v + 1) * LEV, :], first + 2)
         packed = jnp.where((lane >= first) & (lane < first + 4), moved, packed)
     return packed
+
+
+PIECES = (
+    ((4, 0), (5, 3), (6, 12), (7, 15)),
+    ((8, 0), (9, 3), (10, 12), (11, 15)),
+    ((1, 0), (2, 3), (13, 12), (14, 15)),
+)
+
+
+def fold(packed):
+    place = lane_index(FOLD) % 16
+    kept = LEV - FOLD
+    last = packed[kept:, :]
+    parts = []
+    for i, piece in enumerate(PIECES):
+        part = packed[i * FOLD : (i + 1) * FOLD, :]
+        for used, free in piece:
+            part = jnp.where(place == free, roll(last, free - used), part)
+        parts.append(part)
+    return jnp.concatenate(parts + [packed[len(PIECES) * FOLD : kept, :]], axis=0)
+
+
+def unfold(folded):
+    place = lane_index(FOLD) % 16
+    last = jnp.zeros((FOLD, LANES), jnp.float32)
+    for i, piece in enumerate(PIECES):
+        part = folded[i * FOLD : (i + 1) * FOLD, :]
+        for used, free in piece:
+            last = jnp.where(place == used, roll(part, used - free), last)
+    return jnp.concatenate([folded, last], axis=0)
 
 
 def own_kernel(x_ref, diff_ref, edge_ref, surf_ref, spread_ref):
@@ -84,7 +120,7 @@
     packed = edge_lanes(decode(link_ref, 0, link_step), 0, edge_ref[...], lane)
     packed = edge_lanes(decode(mate_ref, 1, mate_step), 3, packed, lane)
     full_ref[...] = packed
-    send_ref[...] = packed.astype(jnp.bfloat16)
+    send_ref[...] = fold(packed).astype(jnp.bfloat16)
     for r in range(2):
         rows, others = [], []
         for v in range(VARS):
@@ -103,21 +139,14 @@
     return jnp.where(place == 1, roll(x, -1), jnp.where(place == 2, roll(x, 1), x))
 
 
-def first_substep(
-    x_ref, link_ref, mate_ref, full_ref, halo, spread_ref, op_ref, out_ref, rhs
-):
+def interior_kernel(x_ref, link_ref, mate_ref, spread_ref, near_ref, rows_ref, rate_ref):
+    del near_ref
     link_step, mate_step = step_of(link_ref), step_of(mate_ref)
     lane = lane_index(LEV)
-    place = lane % 4
-    own = full_ref[...]
-    spread = jnp.zeros((LEV, LANES), jnp.float32)
-    for v in range(VARS):
-        spread = jnp.where(lane // 16 == v, spread_ref[v * LEV : (v + 1) * LEV, :], spread)
-    beside = jnp.where(place == 1, roll(halo, 1) + roll(own, -1), roll(own, 1) + roll(halo, -1))
-    corner = halo + spread * (roll(halo, 4) + roll(halo, -4) + beside - 4.0 * halo)
-    corner = swap_inner(corner, place)
-    halo = swap_inner(halo, place)
-
+    rates = jnp.zeros((LEV, LANES), jnp.float32)
+    for v in range(VARS):
+        rates = jnp.where(lane // 16 == v, spread_ref[v * LEV : (v + 1) * LEV, :], rates)
+    rate_ref[...] = rates
     for v in range(VARS):
         block = slice(v * LEV, (v + 1) * LEV)
         field = [
@@ -131,10 +160,28 @@
         rate = spread_ref[block, :]
         for ri in range(4):
             center = field[ri + 1]
-            ends = roll(halo, 126 - 16 * v - 4 * ri)
-            left = jnp.where(lane == 0, ends, roll(center, 1))
-            right = jnp.where(lane == LANES - 1, ends, roll(center, -1))
-            center = center + rate * (field[ri + 2] + field[ri] + right + left - 4.0 * center)
+            left = jnp.where(lane == 0, 0.0, roll(center, 1))
+            right = jnp.where(lane == LANES - 1, 0.0, roll(center, -1))
+            rows_ref[ri, block, :] = center + rate * (
+                field[ri + 2] + field[ri] + right + left - 4.0 * center
+            )
+
+
+def first_kernel(rows_ref, full_ref, recv_ref, rate_ref, op_ref, out_ref, rhs):
+    lane = lane_index(LEV)
+    place = lane % 4
+    halo = unfold(recv_ref[...].astype(jnp.float32))
+    own = full_ref[...]
+    beside = jnp.where(place == 1, roll(halo, 1) + roll(own, -1), roll(own, 1) + roll(halo, -1))
+    corner = halo + rate_ref[...] * (roll(halo, 4) + roll(halo, -4) + beside - 4.0 * halo)
+    corner = swap_inner(corner, place)
+    halo = swap_inner(halo * rate_ref[...], place)
+    ends = (lane == 0) | (lane == LANES - 1)
+    for v in range(VARS):
+        block = slice(v * LEV, (v + 1) * LEV)
+        for ri in range(4):
+            beyond = jnp.where(ends, roll(halo, 126 - 16 * v - 4 * ri), 0.0)
+            center = rows_ref[ri, block, :] + beyond
             out_ref[ri, block, :] = center
             rhs[block, ri * LANES : (ri + 1) * LANES] = center.astype(jnp.bfloat16)
         moved = roll(corner, -16 * v)
@@ -158,8 +205,14 @@
     return block[at - low : at - low + LEV, :] * step
 
 
-def second_substep(field_ref, spread_ref, op_ref, out_ref, rhs, fluxes, out_hbm, sems):
-    lane = lane_index(LEV)
+def second_kernel(
+    field_ref, spread_ref, op_ref, weight_ref, near_ref, far_ref, entry_ref, pick_ref, count_ref,
+    out_hbm, rhs, out_ref, sems,
+):
+    lane = lane_index(LEV)
+    fluxes = [
+        flux_of(r, weight_ref, near_ref, far_ref, entry_ref, pick_ref, count_ref) for r in range(2)
+    ]
     place = side()
     for v in range(VARS):
         block = slice(v * LEV, (v + 1) * LEV)
@@ -197,46 +250,21 @@
         copy.wait()
 
 
-def flux_of(weight_ref, near_ref, far_ref, entry_ref, pick_ref, count_ref):
+def flux_of(r, weight_ref, near_ref, far_ref, entry_ref, pick_ref, count_ref):
     mine = lax.axis_index("sec")
-    place = side()
-    fluxes = []
-    for r in range(2):
-        blocks, weights = [], []
-        for slot in range(4):
-            entry = entry_ref[0, r, 0, slot]
-            apart = mine ^ (entry // 6)
-            within = entry % 6
-            within = jnp.where(place == 0, within, 5 - within)
-            block = jnp.where(
-                apart == 2, near_ref[within], far_ref[jnp.where(apart == 3, 6, 0) + within]
-            )
-            blocks.append(jnp.where(slot < count_ref[0, r, 0], block, jnp.zeros_like(block)))
-            weights.append(weight_ref[pick_ref[0, r, 0, slot]])
-        fluxes.append(
-            0.5
-            * jnp.dot(
-                jnp.concatenate(blocks, axis=1),
-                jnp.concatenate(weights, axis=0),
-                preferred_element_type=jnp.float32,
-            )
+    blocks, weights = [], []
+    for slot in range(4):
+        entry = entry_ref[0, r, 0, slot]
+        apart = mine ^ (entry // 6)
+        within = entry % 6
+        within = jnp.where(side() == 0, within, 5 - within)
+        block = jnp.where(
+            apart == 2, near_ref[within], far_ref[jnp.where(apart == 3, 6, 0) + within]
         )
-    return fluxes
-
-
-def first_kernel(
-    x_ref, link_ref, mate_ref, full_ref, recv_ref, spread_ref, op_ref, near_rows, rhs
-):
-    halo = recv_ref[...].astype(jnp.float32)
-    first_substep(x_ref, link_ref, mate_ref, full_ref, halo, spread_ref, op_ref, near_rows, rhs)
-
-
-def second_kernel(
-    near_rows, spread_ref, op_ref, weight_ref, near_ref, far_ref, entry_ref, pick_ref, count_ref,
-    out_hbm, rhs, out_ref, sems,
-):
-    fluxes = flux_of(weight_ref, near_ref, far_ref, entry_ref, pick_ref, count_ref)
-    second_substep(near_rows, spread_ref, op_ref, out_ref, rhs, fluxes, out_hbm, sems)
+        blocks.append(jnp.where(slot < count_ref[0, r, 0], block, jnp.zeros_like(block)))
+        weights.append(weight_ref[pick_ref[0, r, 0, slot]])
+    blocks, weights = jnp.concatenate(blocks, axis=1), jnp.concatenate(weights, axis=0)
+    return 0.5 * jnp.dot(blocks, weights, preferred_element_type=jnp.float32)
 
 
 def call(kernel, outs, specs, scratch=(), flops=0, moved=0, out_specs=None):
@@ -268,10 +296,15 @@
 
     def shards(state, column_op, diffusion, remap_weights, source_rows, weight_index, counts):
         x = state.reshape(2 * VL, LANES)
-        wide, narrow = ((LEV, LANES), jnp.float32), ((LEV, LANES), jnp.bfloat16)
-        (msg,) = call(encode_kernel, [((2 * VL + TAIL, LANES), jnp.int16)], [VMEM], moved=10**6)(x)
-        link = send(msg, lambda s, t, c: (s, (t - 1 + 2 * (t % 2)) % tiles, c))
-        mate = send(msg, lambda s, t, c: (s, t + 1 - 2 * (t % 2), c))
+        wide, narrow = ((LEV, LANES), jnp.float32), ((LEV - FOLD, LANES), jnp.bfloat16)
+        to_link, to_mate = call(
+            encode_kernel,
+            [((2 * VL + 2 * TAIL, LANES), jnp.int16), ((2 * VL + TAIL, LANES), jnp.int16)],
+            [VMEM],
+            moved=10**6,
+        )(x)
+        link = send(to_link, lambda s, t, c: (s, (t - 1 + 2 * (t % 2)) % tiles, c))
+        mate = send(to_mate, lambda s, t, c: (s, t + 1 - 2 * (t % 2), c))
         edge, surf, spread = call(
             own_kernel,
             [wide, ((2, VARS, LANES), jnp.float32), ((VL, LANES), jnp.float32)],
@@ -288,14 +321,20 @@
         recv = send(full16, lambda s, t, c: (s, t, 1 - c))
         both = jnp.concatenate([table, near], axis=0)
         far = send(both, lambda s, t, c: (s ^ 1, t, c))
+        inner, rates = call(
+            interior_kernel,
+            [((4, VL, LANES), jnp.float32), wide],
+            [VMEM] * 5,
+            moved=3 * 10**6,
+        )(x, link, mate, spread, near)
         (rows,) = call(
             first_kernel,
             [((5, VL, LANES), jnp.float32)],
-            [VMEM] * 7,
+            [VMEM] * 5,
             [pltpu.VMEM((VL, 5 * LANES), jnp.bfloat16)],
             flops=2 * VL * VL * 5 * LANES,
             moved=2 * 10**6,
-        )(x, link, mate, full, recv, spread, column_op)
+        )(inner, full, recv, rates, column_op)
         (out,) = call(
             second_kernel,
             [((2 * VL, LANES), jnp.float32)],

time: 45.2 us -> 45 us (level)
  waiting for transfers between devices: 5.33 us -> 4.61 us
    ppermute x5, waiting for transfers between devices: 5.33 us -> 4.61 us  [send(): return lax.ppermute(x, AXES, pairs)]
    pallas_call x2 -> x3, Pallas kernels: 1.84 us -> 2.2 us  [the longest x1 1.23 us: shards(): call(first_kernel, [((5, VL, LANES), jnp.float32)], [VMEM] * 5, [pltpu.VM...]
  transfers between devices with their start and end apart: 5 -> 5, of which waited for: 2 -> 3; matrix products, arithmetic and copies ran while one was open for 0% -> 0% of each run, Pallas kernels for 4% -> 5%
where the time goes in v3:
time: 45 us; the launch traced here: 44.1 us
  starting transfers between devices  32.4 us (72%)
  Pallas kernels  5.08 us (11%)
  waiting for transfers between devices  4.61 us (10%)
  local copies, waits for them, and re-layouts  1.87 us (4%)
    ppermute x5, starting transfers between devices, send(): return lax.ppermute(x, AXES, pairs)  32.4 us
    ppermute x5, waiting for transfers between devices, send(): return lax.ppermute(x, AXES, pairs)  4.61 us
    pallas_call x1, Pallas kernels, shards(): call(second_kernel, [((2 * VL, LANES), jnp.float32)], [VMEM] * 6 + [SMEM]...  2.28 us
    unnamed x17, local copies, waits for them, and re-layouts  1.87 us
    pallas_call x1, Pallas kernels, shards(): call(first_kernel, [((5, VL, LANES), jnp.float32)], [VMEM] * 5, [pltpu.VM...  1.23 us
  transfers between devices with their start and end apart: 5, of which 3 were waited for; matrix products, arithmetic and copies ran while one was open for 0% of the time, Pallas kernels for 5%

profile of v3, /device:TPU:14, one launch (start us, length us, event | category | flops | bytes accessed | tf_op | source)
XLA Modules:
  0.0 44.1 jit_solution(16072682371889295455)
XLA Ops:
  0.0 0.0 copy-start.7
  0.0 0.0 copy-start
  0.0 1.1 %copy-done = f32[1,8,72,2,128]{4,3,2,1,0:T(2,128)S(1)} copy-done((f32[1,8,72,2,128]{4,3,2,1,0:T(2,128)S(1)}, f32[1,8,72,2,128]{4,3,2,1,0:T(2,128)}, u32[]{:S(2)}) %copy-start) | copy-done | bytes 589848
  1.1 0.0 copy-start.1
  1.1 0.3 shard_map.73
  1.4 0.0 copy-start.2
  1.4 20.6 %collective-permute-start = (s16[1184,128]{1,0:T(8,128)(2,1)S(1)}, s16[1184,128]{1,0:T(8,128)(2,1)S(1)}, u32[]{:S(2)}, u32[]{:S(2)}) collective-permute-start(s16[1184,128]{1,0:T(8,128)(2,1)S(1)} %get-tuple-element.15), channel_id=1, source_target_pairs={{0,254},{1,255},{2,4},{3,5},{4,2},{5,3},{6,8},{7,9},{8,6},{9,7},{1... | collective-permute-start | bytes 909320 | tf_op jit(solution)/shard_map/ppermute | solution.py:295
  22.0 1.9 %collective-permute-start.1 = (s16[1168,128]{1,0:T(8,128)(2,1)S(1)}, s16[1168,128]{1,0:T(8,128)(2,1)S(1)}, u32[]{:S(2)}, u32[]{:S(2)}) collective-permute-start(s16[1168,128]{1,0:T(8,128)(2,1)S(1)} %get-tuple-element.16), channel_id=1, source_target_pairs={{0,2},{1,3},{2,0},{3,1},{4,6},{5,7},{6,4},{7,5},{8,10},{9,11},{10,... | collective-permute-start | bytes 897032 | tf_op jit(solution)/shard_map/ppermute | solution.py:295
  23.9 0.0 copy-start.4
  23.9 0.7 %copy-done.4 = f32[1,576]{1,0:T(1,128)S(1)} copy-done((f32[1,576]{1,0:T(1,128)S(1)}, f32[1,576]{1,0:T(1,128)}, u32[]{:S(2)}) %copy-start.4) | copy-done | bytes 2328
  24.6 0.3 shard_map.74
  24.9 0.5 %collective-permute-done.1.mate_ref = s16[1168,128]{1,0:T(8,128)(2,1)S(1)} collective-permute-done((s16[1168,128]{1,0:T(8,128)(2,1)S(1)}, s16[1168,128]{1,0:T(8,128)(2,1)S(1)}, u32[]{:S(2)}, u32[]{:S(2)}) %collective-permute-start.1) | collective-permute-done | bytes 299040 | tf_op jit(solution)/shard_map/ppermute | solution.py:295
  25.5 1.0 %collective-permute-done.link_ref = s16[1184,128]{1,0:T(8,128)(2,1)S(1)} collective-permute-done((s16[1184,128]{1,0:T(8,128)(2,1)S(1)}, s16[1184,128]{1,0:T(8,128)(2,1)S(1)}, u32[]{:S(2)}, u32[]{:S(2)}) %collective-permute-start) | collective-permute-done | bytes 303136 | tf_op jit(solution)/shard_map/ppermute | solution.py:295
  26.5 0.3 shard_map.75
  26.7 4.2 %collective-permute-start.2 = (bf16[6,8,128]{2,1,0:T(8,128)(2,1)S(1)}, bf16[6,8,128]{2,1,0:T(8,128)(2,1)S(1)}, u32[]{:S(2)}, u32[]{:S(2)}) collective-permute-start(bf16[6,8,128]{2,1,0:T(8,128)(2,1)S(1)} %get-tuple-element.20), channel_id=1, source_target_pairs={{0,512},{1,513},{2,514},{3,515},{4,516},{5,517},{6,518},{7,519},{8... | collective-permute-start | bytes 36872 | tf_op jit(solution)/shard_map/ppermute | solution.py:295
  31.0 0.0 copy-done.7
  31.0 0.1 copy.8.count_ref
  31.1 3.2 %collective-permute-start.3 = (bf16[56,128]{1,0:T(8,128)(2,1)S(1)}, bf16[56,128]{1,0:T(8,128)(2,1)S(1)}, u32[]{:S(2)}, u32[]{:S(2)}) collective-permute-start(bf16[56,128]{1,0:T(8,128)(2,1)S(1)} %get-tuple-element.23), channel_id=1, source_target_pairs={{0,1},{1,0},{2,3},{3,2},{4,5},{5,4},{6,7},{7,6},{8,9},{9,8},{10,11... | collective-permute-start | bytes 43016 | tf_op jit(solution)/shard_map/ppermute | solution.py:295
  34.3 0.0 collective-permute-done.2.near_ref
  34.3 2.4 %collective-permute-start.4 = (bf16[12,8,128]{2,1,0:T(8,128)(2,1)S(1)}, bf16[12,8,128]{2,1,0:T(8,128)(2,1)S(1)}, u32[]{:S(2)}, u32[]{:S(2)}) collective-permute-start(bf16[12,8,128]{2,1,0:T(8,128)(2,1)S(1)} %pad_maximum_fusion), channel_id=1, source_target_pairs={{0,256},{1,257},{2,258},{3,259},{4,260},{5,261},{6,262},{7,263},{8... | collective-permute-start | bytes 73736 | tf_op jit(solution)/shard_map/ppermute | solution.py:295
  36.8 0.0 copy-done.1
  36.8 0.7 %shard_map.76 = (f32[4,576,128]{2,1,0:T(8,128)S(1)}, f32[72,128]{1,0:T(8,128)S(1)}) custom-call(f32[1152,128]{1,0:T(8,128)S(1)} %bitcast.4, s16[1184,128]{1,0:T(8,128)(2,1)S(1)} %collective-permute-done.link_ref, s16[1168,128]{1,0:T(8,128)(2,1)S(1)} %collective-permute-done.1.mate_ref, f32[576,128]{1,0:T(8,128)S(1)} %get-tuple-element.17.spread_ref, ...), custom_call_target="tpu_custom_call" | custom-call | bytes 3000000 | tf_op jit(solution)/shard_map/pallas_call | solution.py:324
  37.5 3.1 %collective-permute-done.3.recv_ref = bf16[56,128]{1,0:T(8,128)(2,1)S(1)} collective-permute-done((bf16[56,128]{1,0:T(8,128)(2,1)S(1)}, bf16[56,128]{1,0:T(8,128)(2,1)S(1)}, u32[]{:S(2)}, u32[]{:S(2)}) %collective-permute-start.3) | collective-permute-done | bytes 14368 | tf_op jit(solution)/shard_map/ppermute | solution.py:295
  40.6 0.0 copy-done.2
  40.6 0.0 copy-start.3
  40.6 0.0 copy-start.5
  40.6 1.2 %shard_map.77.field_ref = f32[5,576,128]{2,1,0:T(8,128)S(1)} custom-call(f32[4,576,128]{2,1,0:T(8,128)S(1)} %get-tuple-element.21.rows_ref, f32[72,128]{1,0:T(8,128)S(1)} %get-tuple-element.22.full_ref, bf16[56,128]{1,0:T(8,128)(2,1)S(1)} %collective-permute-done.3.recv_ref, f32[72,128]{1,0:T(8,128)S(1)} %get-tuple-element.24.rate_ref, ...), custom_call_target="tpu_custom_call" | custom-call | flops 424673280 | bytes 2000000 | tf_op jit(solution)/shard_map/pallas_call | solution.py:330
  41.8 0.0 collective-permute-done.4.far_ref
  41.8 0.0 copy-done.3
  41.8 0.0 copy-done.5
  41.8 0.0 copy-done.6
  41.9 2.3 %shard_map.78 = f32[1152,128]{1,0:T(8,128)} custom-call(f32[5,576,128]{2,1,0:T(8,128)S(1)} %shard_map.77.field_ref, f32[576,128]{1,0:T(8,128)S(1)} %get-tuple-element.17.spread_ref, bf16[1,576,576]{2,1,0:T(8,128)(2,1)S(1)} %copy-done.2, bf16[32,128,128]{2,1,0:T(8,128)(2,1)S(1)} %copy-done.3, bf16[6,8,128]{2,1,0:T(8,128)(2,1)S(1)} %collective-permute-done.2.near_ref, ...), custom_call_target="tpu_custom_call" | custom-call | flops 169869312 | bytes 2000000 | tf_op jit(solution)/shard_map/pallas_call | solution.py:338
  (2 shorter events, 0.0 us)
Async XLA Ops:
  0.0 31.0 %copy-start.7 = (s32[1,2,1]{1,2,0:T(1,128)S(1)}, s32[1,2,1]{1,2,0:T(1,128)}, u32[]{:S(2)}) copy-start(s32[1,2,1]{1,2,0:T(1,128)} %param.13) | copy-start | bytes 28
  0.0 1.1 %copy-start = (f32[1,8,72,2,128]{4,3,2,1,0:T(2,128)S(1)}, f32[1,8,72,2,128]{4,3,2,1,0:T(2,128)}, u32[]{:S(2)}) copy-start(f32[1,8,72,2,128]{4,3,2,1,0:T(2,128)} %param.7) | copy-start | bytes 1769476
  1.1 35.7 %copy-start.1 = (f32[1,8,72,2,128]{4,3,2,1,0:T(2,128)S(1)}, f32[1,8,72,2,128]{4,3,2,1,0:T(2,128)}, u32[]{:S(2)}) copy-start(f32[1,8,72,2,128]{4,3,2,1,0:T(2,128)} %param.7) | copy-start | bytes 1769476
  1.4 39.2 %copy-start.2 = (bf16[1,576,576]{2,1,0:T(8,128)(2,1)S(1)}, bf16[1,576,576]{2,1,0:T(8,128)(2,1)}, u32[]{:S(2)}) copy-start(bf16[1,576,576]{2,1,0:T(8,128)(2,1)} %op_ref.3) | copy-start | bytes 1990660
  1.4 25.1 %collective-permute-start = (s16[1184,128]{1,0:T(8,128)(2,1)S(1)}, s16[1184,128]{1,0:T(8,128)(2,1)S(1)}, u32[]{:S(2)}, u32[]{:S(2)}) collective-permute-start(s16[1184,128]{1,0:T(8,128)(2,1)S(1)} %get-tuple-element.15), channel_id=1, source_target_pairs={{0,254},{1,255},{2,4},{3,5},{4,2},{5,3},{6,8},{7,9},{8,6},{9,7},{1... | collective-permute-start | bytes 909320 | tf_op jit(solution)/shard_map/ppermute | solution.py:295
  22.0 3.5 %collective-permute-start.1 = (s16[1168,128]{1,0:T(8,128)(2,1)S(1)}, s16[1168,128]{1,0:T(8,128)(2,1)S(1)}, u32[]{:S(2)}, u32[]{:S(2)}) collective-permute-start(s16[1168,128]{1,0:T(8,128)(2,1)S(1)} %get-tuple-element.16), channel_id=1, source_target_pairs={{0,2},{1,3},{2,0},{3,1},{4,6},{5,7},{6,4},{7,5},{8,10},{9,11},{10,... | collective-permute-start | bytes 897032 | tf_op jit(solution)/shard_map/ppermute | solution.py:295
  23.9 0.7 %copy-start.4 = (f32[1,576]{1,0:T(1,128)S(1)}, f32[1,576]{1,0:T(1,128)}, u32[]{:S(2)}) copy-start(f32[1,576]{1,0:T(1,128)} %diff_ref.1) | copy-start | bytes 6916
  26.7 7.6 %collective-permute-start.2 = (bf16[6,8,128]{2,1,0:T(8,128)(2,1)S(1)}, bf16[6,8,128]{2,1,0:T(8,128)(2,1)S(1)}, u32[]{:S(2)}, u32[]{:S(2)}) collective-permute-start(bf16[6,8,128]{2,1,0:T(8,128)(2,1)S(1)} %get-tuple-element.20), channel_id=1, source_target_pairs={{0,512},{1,513},{2,514},{3,515},{4,516},{5,517},{6,518},{7,519},{8... | collective-permute-start | bytes 36872 | tf_op jit(solution)/shard_map/ppermute | solution.py:295
  31.1 9.5 %collective-permute-start.3 = (bf16[56,128]{1,0:T(8,128)(2,1)S(1)}, bf16[56,128]{1,0:T(8,128)(2,1)S(1)}, u32[]{:S(2)}, u32[]{:S(2)}) collective-permute-start(bf16[56,128]{1,0:T(8,128)(2,1)S(1)} %get-tuple-element.23), channel_id=1, source_target_pairs={{0,1},{1,0},{2,3},{3,2},{4,5},{5,4},{6,7},{7,6},{8,9},{9,8},{10,11... | collective-permute-start | bytes 43016 | tf_op jit(solution)/shard_map/ppermute | solution.py:295
  34.3 7.5 %collective-permute-start.4 = (bf16[12,8,128]{2,1,0:T(8,128)(2,1)S(1)}, bf16[12,8,128]{2,1,0:T(8,128)(2,1)S(1)}, u32[]{:S(2)}, u32[]{:S(2)}) collective-permute-start(bf16[12,8,128]{2,1,0:T(8,128)(2,1)S(1)} %pad_maximum_fusion), channel_id=1, source_target_pairs={{0,256},{1,257},{2,258},{3,259},{4,260},{5,261},{6,262},{7,263},{8... | collective-permute-start | bytes 73736 | tf_op jit(solution)/shard_map/ppermute | solution.py:295
  40.6 1.3 %copy-start.3 = (bf16[32,128,128]{2,1,0:T(8,128)(2,1)S(1)}, bf16[32,128,128]{2,1,0:T(8,128)(2,1)}, u32[]{:S(2)}) copy-start(bf16[32,128,128]{2,1,0:T(8,128)(2,1)} %weight_ref.1) | copy-start | bytes 3145732
  40.6 1.3 %copy-start.5 = (s32[1,2,1,4]{3,2,1,0:T(1,128)S(1)}, s32[1,2,1,4]{3,2,1,0:T(1,128)}, u32[]{:S(2)}) copy-start(s32[1,2,1,4]{3,2,1,0:T(1,128)} %entry_ref.1) | copy-start | bytes 100
  40.6 1.3 %copy-start.6 = (s32[1,2,1,4]{3,2,1,0:T(1,128)S(1)}, s32[1,2,1,4]{3,2,1,0:T(1,128)}, u32[]{:S(2)}) copy-start(s32[1,2,1,4]{3,2,1,0:T(1,128)} %pick_ref.1) | copy-start | bytes 100

commit v4 on v3

--- a/solution.py
+++ b/solution.py
@@ -11,6 +11,7 @@
 LANES = 128
 TAIL = 16
 FOLD = 16
+PARTS = ((0, 4), (4, 6), (6, 8))
 TOP = 32767.0
 AXES = ("sec", "tile", "col")
 VMEM = pl.BlockSpec(memory_space=pltpu.VMEM)
@@ -167,7 +168,9 @@
             )
 
 
-def first_kernel(rows_ref, full_ref, recv_ref, rate_ref, op_ref, out_ref, rhs):
+def first_kernel(
+    rows_ref, full_ref, recv_ref, rate_ref, spread_ref, op_ref, center_ref, rounded_ref, rhs, out_ref
+):
     lane = lane_index(LEV)
     place = lane % 4
     halo = unfold(recv_ref[...].astype(jnp.float32))
@@ -196,6 +199,7 @@
         )
         for k in range(width):
             out_ref[ri + k] += tendency[:, k * LANES : (k + 1) * LANES]
+    second_stencil(out_ref, spread_ref, center_ref, rounded_ref)
 
 
 def decode_block(msg_ref, r, v, step):
@@ -205,14 +209,8 @@
     return block[at - low : at - low + LEV, :] * step
 
 
-def second_kernel(
-    field_ref, spread_ref, op_ref, weight_ref, near_ref, far_ref, entry_ref, pick_ref, count_ref,
-    out_hbm, rhs, out_ref, sems,
-):
-    lane = lane_index(LEV)
-    fluxes = [
-        flux_of(r, weight_ref, near_ref, far_ref, entry_ref, pick_ref, count_ref) for r in range(2)
-    ]
+def second_stencil(field_ref, spread_ref, center_ref, rounded_ref):
+    lane = lane_index(LEV)
     place = side()
     for v in range(VARS):
         block = slice(v * LEV, (v + 1) * LEV)
@@ -226,26 +224,36 @@
             right = jnp.where(lane == LANES - 1, ends, roll(center, -1))
             center = center + rate * (field[ri + 1] + field[ri - 1] + right + left - 4.0 * center)
             at = 2 * LEV * v + (place if r == 0 else 1 - place)
-            out_ref[pl.ds(at, LEV, stride=2), :] = center
-            rhs[block, r * LANES : (r + 1) * LANES] = center.astype(jnp.bfloat16)
-    half = VL // 2
+            center_ref[pl.ds(at, LEV, stride=2), :] = center
+            rounded_ref[block, r * LANES : (r + 1) * LANES] = center.astype(jnp.bfloat16)
+
+
+def second_kernel(
+    center_ref, rounded_ref, op_ref, weight_ref, near_ref, far_ref, entry_ref, pick_ref, count_ref,
+    out_hbm, out_ref, sems,
+):
+    fluxes = [
+        flux_of(r, weight_ref, near_ref, far_ref, entry_ref, pick_ref, count_ref) for r in range(2)
+    ]
+    place = side()
     copies = []
-    for part in range(2):
+    for i, (low, high) in enumerate(PARTS):
+        size = (high - low) * LEV
         tendency = jnp.dot(
-            op_ref[0, part * half : (part + 1) * half, :],
-            rhs[:, : 2 * LANES],
+            op_ref[0, low * LEV : high * LEV, :],
+            rounded_ref[...],
             preferred_element_type=jnp.float32,
         )
         for r in range(2):
-            rows = pl.ds(2 * half * part + (place if r == 0 else 1 - place), half, stride=2)
-            out_ref[rows, :] += tendency[:, r * LANES : (r + 1) * LANES]
-        for v in range(part * VARS // 2, (part + 1) * VARS // 2):
+            rows = pl.ds(2 * LEV * low + (place if r == 0 else 1 - place), size, stride=2)
+            out_ref[rows, :] = center_ref[rows, :] + tendency[:, r * LANES : (r + 1) * LANES]
+        for v in range(low, high):
             for r in range(2):
                 at = 2 * LEV * v + r
                 out_ref[at : at + 1, :] = out_ref[at : at + 1, :] + fluxes[r][v : v + 1, :]
-        rows = pl.ds(part * VL, VL)
-        copies.append(pltpu.make_async_copy(out_ref.at[rows, :], out_hbm.at[rows, :], sems.at[part]))
-        copies[part].start()
+        rows = pl.ds(2 * LEV * low, 2 * size)
+        copies.append(pltpu.make_async_copy(out_ref.at[rows, :], out_hbm.at[rows, :], sems.at[i]))
+        copies[i].start()
     for copy in copies:
         copy.wait()
 
@@ -327,27 +335,29 @@
             [VMEM] * 5,
             moved=3 * 10**6,
         )(x, link, mate, spread, near)
-        (rows,) = call(
+        center, rounded = call(
             first_kernel,
-            [((5, VL, LANES), jnp.float32)],
-            [VMEM] * 5,
-            [pltpu.VMEM((VL, 5 * LANES), jnp.bfloat16)],
+            [((2 * VL, LANES), jnp.float32), ((VL, 2 * LANES), jnp.bfloat16)],
+            [VMEM] * 6,
+            [
+                pltpu.VMEM((VL, 5 * LANES), jnp.bfloat16),
+                pltpu.VMEM((5, VL, LANES), jnp.float32),
+            ],
             flops=2 * VL * VL * 5 * LANES,
             moved=2 * 10**6,
-        )(inner, full, recv, rates, column_op)
+        )(inner, full, recv, rates, spread, column_op)
         (out,) = call(
             second_kernel,
             [((2 * VL, LANES), jnp.float32)],
             [VMEM] * 6 + [SMEM] * 3,
             [
-                pltpu.VMEM((VL, 2 * LANES), jnp.bfloat16),
                 pltpu.VMEM((2 * VL, LANES), jnp.float32),
-                pltpu.SemaphoreType.DMA((2,)),
+                pltpu.SemaphoreType.DMA((len(PARTS),)),
             ],
             flops=2 * VL * VL * 2 * LANES,
             moved=2 * 10**6,
             out_specs=[HBM],
-        )(rows, spread, column_op, remap_weights, near, far, source_rows, weight_index, counts)
+        )(center, rounded, column_op, remap_weights, near, far, source_rows, weight_index, counts)
         return out.reshape(1, VARS, LEV, 2, LANES)
 
     in_specs = (

time: 45 us -> 44.5 us (0.989)
  transfers between devices with their start and end apart: 5 -> 5, of which waited for: 3 -> 3; matrix products, arithmetic and copies ran while one was open for 0% -> 0% of each run, Pallas kernels for 5% -> 6%
where the time goes in v4:
time: 44.5 us; the launch traced here: 43.8 us
  starting transfers between devices  32.3 us (73%)
  Pallas kernels  4.93 us (11%)
  waiting for transfers between devices  4.56 us (10%)
  local copies, waits for them, and re-layouts  1.88 us (4%)
    ppermute x5, starting transfers between devices, send(): return lax.ppermute(x, AXES, pairs)  32.3 us
    ppermute x5, waiting for transfers between devices, send(): return lax.ppermute(x, AXES, pairs)  4.56 us
    pallas_call x1, Pallas kernels, shards(): call(second_kernel, [((2 * VL, LANES), jnp.float32)], [VMEM] * 6 + [SMEM]...  1.9 us
    unnamed x17, local copies, waits for them, and re-layouts  1.88 us
    pallas_call x1, Pallas kernels, shards(): call(first_kernel, [((2 * VL, LANES), jnp.float32), ((VL, 2 * LANES), jnp...  1.46 us
  transfers between devices with their start and end apart: 5, of which 3 were waited for; matrix products, arithmetic and copies ran while one was open for 0% of the time, Pallas kernels for 6%

profile of v4, /device:TPU:14, one launch (start us, length us, event | category | flops | bytes accessed | tf_op | source)
XLA Modules:
  0.0 43.8 jit_solution(2186764930994602315)
XLA Ops:
  0.0 0.0 copy-start.7
  0.0 0.0 copy-start
  0.0 1.1 %copy-done = f32[1,8,72,2,128]{4,3,2,1,0:T(2,128)S(1)} copy-done((f32[1,8,72,2,128]{4,3,2,1,0:T(2,128)S(1)}, f32[1,8,72,2,128]{4,3,2,1,0:T(2,128)}, u32[]{:S(2)}) %copy-start) | copy-done | bytes 589848
  1.1 0.3 shard_map.73
  1.4 20.5 %collective-permute-start = (s16[1184,128]{1,0:T(8,128)(2,1)S(1)}, s16[1184,128]{1,0:T(8,128)(2,1)S(1)}, u32[]{:S(2)}, u32[]{:S(2)}) collective-permute-start(s16[1184,128]{1,0:T(8,128)(2,1)S(1)} %get-tuple-element.17), channel_id=1, source_target_pairs={{0,254},{1,255},{2,4},{3,5},{4,2},{5,3},{6,8},{7,9},{8,6},{9,7},{1... | collective-permute-start | bytes 909320 | tf_op jit(solution)/shard_map/ppermute | solution.py:303
  21.8 1.9 %collective-permute-start.1 = (s16[1168,128]{1,0:T(8,128)(2,1)S(1)}, s16[1168,128]{1,0:T(8,128)(2,1)S(1)}, u32[]{:S(2)}, u32[]{:S(2)}) collective-permute-start(s16[1168,128]{1,0:T(8,128)(2,1)S(1)} %get-tuple-element.18), channel_id=1, source_target_pairs={{0,2},{1,3},{2,0},{3,1},{4,6},{5,7},{6,4},{7,5},{8,10},{9,11},{10,... | collective-permute-start | bytes 897032 | tf_op jit(solution)/shard_map/ppermute | solution.py:303
  23.8 0.0 copy-start.4
  23.8 0.7 %copy-done.4 = f32[1,576]{1,0:T(1,128)S(1)} copy-done((f32[1,576]{1,0:T(1,128)S(1)}, f32[1,576]{1,0:T(1,128)}, u32[]{:S(2)}) %copy-start.4) | copy-done | bytes 2328
  24.4 0.3 shard_map.74
  24.8 0.0 copy-start.2
  24.8 0.5 %collective-permute-done.1.mate_ref = s16[1168,128]{1,0:T(8,128)(2,1)S(1)} collective-permute-done((s16[1168,128]{1,0:T(8,128)(2,1)S(1)}, s16[1168,128]{1,0:T(8,128)(2,1)S(1)}, u32[]{:S(2)}, u32[]{:S(2)}) %collective-permute-start.1) | collective-permute-done | bytes 299040 | tf_op jit(solution)/shard_map/ppermute | solution.py:303
  25.3 1.0 %collective-permute-done.link_ref = s16[1184,128]{1,0:T(8,128)(2,1)S(1)} collective-permute-done((s16[1184,128]{1,0:T(8,128)(2,1)S(1)}, s16[1184,128]{1,0:T(8,128)(2,1)S(1)}, u32[]{:S(2)}, u32[]{:S(2)}) %collective-permute-start) | collective-permute-done | bytes 303136 | tf_op jit(solution)/shard_map/ppermute | solution.py:303
  26.3 0.3 shard_map.75
  26.6 4.2 %collective-permute-start.2 = (bf16[6,8,128]{2,1,0:T(8,128)(2,1)S(1)}, bf16[6,8,128]{2,1,0:T(8,128)(2,1)S(1)}, u32[]{:S(2)}, u32[]{:S(2)}) collective-permute-start(bf16[6,8,128]{2,1,0:T(8,128)(2,1)S(1)} %get-tuple-element.22), channel_id=1, source_target_pairs={{0,512},{1,513},{2,514},{3,515},{4,516},{5,517},{6,518},{7,519},{8... | collective-permute-start | bytes 36872 | tf_op jit(solution)/shard_map/ppermute | solution.py:303
  30.8 0.0 copy-done.7
  30.8 0.1 copy.8.count_ref
  30.9 3.2 %collective-permute-start.3 = (bf16[56,128]{1,0:T(8,128)(2,1)S(1)}, bf16[56,128]{1,0:T(8,128)(2,1)S(1)}, u32[]{:S(2)}, u32[]{:S(2)}) collective-permute-start(bf16[56,128]{1,0:T(8,128)(2,1)S(1)} %get-tuple-element.25), channel_id=1, source_target_pairs={{0,1},{1,0},{2,3},{3,2},{4,5},{5,4},{6,7},{7,6},{8,9},{9,8},{10,11... | collective-permute-start | bytes 43016 | tf_op jit(solution)/shard_map/ppermute | solution.py:303
  34.2 0.0 collective-permute-done.2.near_ref
  34.2 2.4 %collective-permute-start.4 = (bf16[12,8,128]{2,1,0:T(8,128)(2,1)S(1)}, bf16[12,8,128]{2,1,0:T(8,128)(2,1)S(1)}, u32[]{:S(2)}, u32[]{:S(2)}) collective-permute-start(bf16[12,8,128]{2,1,0:T(8,128)(2,1)S(1)} %pad_maximum_fusion), channel_id=1, source_target_pairs={{0,256},{1,257},{2,258},{3,259},{4,260},{5,261},{6,262},{7,263},{8... | collective-permute-start | bytes 73736 | tf_op jit(solution)/shard_map/ppermute | solution.py:303
  36.6 0.0 copy-done.1
  36.7 0.7 %shard_map.76 = (f32[4,576,128]{2,1,0:T(8,128)S(1)}, f32[72,128]{1,0:T(8,128)S(1)}) custom-call(f32[1152,128]{1,0:T(8,128)S(1)} %bitcast.4, s16[1184,128]{1,0:T(8,128)(2,1)S(1)} %collective-permute-done.link_ref, s16[1168,128]{1,0:T(8,128)(2,1)S(1)} %collective-permute-done.1.mate_ref, f32[576,128]{1,0:T(8,128)S(1)} %get-tuple-element.19.spread_ref, ...), custom_call_target="tpu_custom_call" | custom-call | bytes 3000000 | tf_op jit(solution)/shard_map/pallas_call | solution.py:332
  37.4 0.0 copy-start.3
  37.4 0.0 copy-start.5
  37.4 0.0 copy-start.6
  37.4 3.0 %collective-permute-done.3.recv_ref = bf16[56,128]{1,0:T(8,128)(2,1)S(1)} collective-permute-done((bf16[56,128]{1,0:T(8,128)(2,1)S(1)}, bf16[56,128]{1,0:T(8,128)(2,1)S(1)}, u32[]{:S(2)}, u32[]{:S(2)}) %collective-permute-start.3) | collective-permute-done | bytes 14368 | tf_op jit(solution)/shard_map/ppermute | solution.py:303
  40.4 0.0 copy-done.2
  40.4 1.5 %shard_map.77 = (f32[1152,128]{1,0:T(8,128)S(1)}, bf16[576,256]{1,0:T(8,128)(2,1)S(1)}) custom-call(f32[4,576,128]{2,1,0:T(8,128)S(1)} %get-tuple-element.23.rows_ref, f32[72,128]{1,0:T(8,128)S(1)} %get-tuple-element.24.full_ref, bf16[56,128]{1,0:T(8,128)(2,1)S(1)} %collective-permute-done.3.recv_ref, f32[72,128]{1,0:T(8,128)S(1)} %get-tuple-element.26.rate_ref, ...), custom_call_target="tpu_custom_call" | custom-call | flops 424673280 | bytes 2000000 | tf_op jit(solution)/shard_map/pallas_call | solution.py:338
  41.9 0.0 collective-permute-done.4.far_ref
  41.9 0.0 copy-done.3
  41.9 0.0 copy-done.5
  41.9 0.0 copy-done.6
  41.9 1.9 %shard_map.78 = f32[1152,128]{1,0:T(8,128)} custom-call(f32[1152,128]{1,0:T(8,128)S(1)} %get-tuple-element.27.center_ref, bf16[576,256]{1,0:T(8,128)(2,1)S(1)} %get-tuple-element.28.rounded_ref, bf16[1,576,576]{2,1,0:T(8,128)(2,1)S(1)} %copy-done.2, bf16[32,128,128]{2,1,0:T(8,128)(2,1)S(1)} %copy-done.3, ...), custom_call_target="tpu_custom_call" | custom-call | flops 169869312 | bytes 2000000 | tf_op jit(solution)/shard_map/pallas_call | solution.py:349
  (2 shorter events, 0.0 us)
Async XLA Ops:
  0.0 30.8 %copy-start.7 = (s32[1,2,1]{1,2,0:T(1,128)S(1)}, s32[1,2,1]{1,2,0:T(1,128)}, u32[]{:S(2)}) copy-start(s32[1,2,1]{1,2,0:T(1,128)} %param.13) | copy-start | bytes 28
  0.0 1.1 %copy-start = (f32[1,8,72,2,128]{4,3,2,1,0:T(2,128)S(1)}, f32[1,8,72,2,128]{4,3,2,1,0:T(2,128)}, u32[]{:S(2)}) copy-start(f32[1,8,72,2,128]{4,3,2,1,0:T(2,128)} %param.7) | copy-start | bytes 1769476
  1.1 35.6 %copy-start.1 = (f32[1,8,72,2,128]{4,3,2,1,0:T(2,128)S(1)}, f32[1,8,72,2,128]{4,3,2,1,0:T(2,128)}, u32[]{:S(2)}) copy-start(f32[1,8,72,2,128]{4,3,2,1,0:T(2,128)} %param.7) | copy-start | bytes 1769476
  1.4 24.9 %collective-permute-start = (s16[1184,128]{1,0:T(8,128)(2,1)S(1)}, s16[1184,128]{1,0:T(8,128)(2,1)S(1)}, u32[]{:S(2)}, u32[]{:S(2)}) collective-permute-start(s16[1184,128]{1,0:T(8,128)(2,1)S(1)} %get-tuple-element.17), channel_id=1, source_target_pairs={{0,254},{1,255},{2,4},{3,5},{4,2},{5,3},{6,8},{7,9},{8,6},{9,7},{1... | collective-permute-start | bytes 909320 | tf_op jit(solution)/shard_map/ppermute | solution.py:303
  21.8 3.5 %collective-permute-start.1 = (s16[1168,128]{1,0:T(8,128)(2,1)S(1)}, s16[1168,128]{1,0:T(8,128)(2,1)S(1)}, u32[]{:S(2)}, u32[]{:S(2)}) collective-permute-start(s16[1168,128]{1,0:T(8,128)(2,1)S(1)} %get-tuple-element.18), channel_id=1, source_target_pairs={{0,2},{1,3},{2,0},{3,1},{4,6},{5,7},{6,4},{7,5},{8,10},{9,11},{10,... | collective-permute-start | bytes 897032 | tf_op jit(solution)/shard_map/ppermute | solution.py:303
  23.8 0.7 %copy-start.4 = (f32[1,576]{1,0:T(1,128)S(1)}, f32[1,576]{1,0:T(1,128)}, u32[]{:S(2)}) copy-start(f32[1,576]{1,0:T(1,128)} %diff_ref.1) | copy-start | bytes 6916
  24.8 15.7 %copy-start.2 = (bf16[1,576,576]{2,1,0:T(8,128)(2,1)S(1)}, bf16[1,576,576]{2,1,0:T(8,128)(2,1)}, u32[]{:S(2)}) copy-start(bf16[1,576,576]{2,1,0:T(8,128)(2,1)} %op_ref.3) | copy-start | bytes 1990660
  26.6 7.6 %collective-permute-start.2 = (bf16[6,8,128]{2,1,0:T(8,128)(2,1)S(1)}, bf16[6,8,128]{2,1,0:T(8,128)(2,1)S(1)}, u32[]{:S(2)}, u32[]{:S(2)}) collective-permute-start(bf16[6,8,128]{2,1,0:T(8,128)(2,1)S(1)} %get-tuple-element.22), channel_id=1, source_target_pairs={{0,512},{1,513},{2,514},{3,515},{4,516},{5,517},{6,518},{7,519},{8... | collective-permute-start | bytes 36872 | tf_op jit(solution)/shard_map/ppermute | solution.py:303
  30.9 9.5 %collective-permute-start.3 = (bf16[56,128]{1,0:T(8,128)(2,1)S(1)}, bf16[56,128]{1,0:T(8,128)(2,1)S(1)}, u32[]{:S(2)}, u32[]{:S(2)}) collective-permute-start(bf16[56,128]{1,0:T(8,128)(2,1)S(1)} %get-tuple-element.25), channel_id=1, source_target_pairs={{0,1},{1,0},{2,3},{3,2},{4,5},{5,4},{6,7},{7,6},{8,9},{9,8},{10,11... | collective-permute-start | bytes 43016 | tf_op jit(solution)/shard_map/ppermute | solution.py:303
  34.2 7.7 %collective-permute-start.4 = (bf16[12,8,128]{2,1,0:T(8,128)(2,1)S(1)}, bf16[12,8,128]{2,1,0:T(8,128)(2,1)S(1)}, u32[]{:S(2)}, u32[]{:S(2)}) collective-permute-start(bf16[12,8,128]{2,1,0:T(8,128)(2,1)S(1)} %pad_maximum_fusion), channel_id=1, source_target_pairs={{0,256},{1,257},{2,258},{3,259},{4,260},{5,261},{6,262},{7,263},{8... | collective-permute-start | bytes 73736 | tf_op jit(solution)/shard_map/ppermute | solution.py:303
  37.4 4.5 %copy-start.3 = (bf16[32,128,128]{2,1,0:T(8,128)(2,1)S(1)}, bf16[32,128,128]{2,1,0:T(8,128)(2,1)}, u32[]{:S(2)}) copy-start(bf16[32,128,128]{2,1,0:T(8,128)(2,1)} %weight_ref.1) | copy-start | bytes 3145732
  37.4 4.5 %copy-start.5 = (s32[1,2,1,4]{3,2,1,0:T(1,128)S(1)}, s32[1,2,1,4]{3,2,1,0:T(1,128)}, u32[]{:S(2)}) copy-start(s32[1,2,1,4]{3,2,1,0:T(1,128)} %entry_ref.1) | copy-start | bytes 100
  37.4 4.5 %copy-start.6 = (s32[1,2,1,4]{3,2,1,0:T(1,128)S(1)}, s32[1,2,1,4]{3,2,1,0:T(1,128)}, u32[]{:S(2)}) copy-start(s32[1,2,1,4]{3,2,1,0:T(1,128)} %pick_ref.1) | copy-start | bytes 100

commit v5 on v4

--- a/solution.py
+++ b/solution.py
@@ -269,7 +269,7 @@
         block = jnp.where(
             apart == 2, near_ref[within], far_ref[jnp.where(apart == 3, 6, 0) + within]
         )
-        blocks.append(jnp.where(slot < count_ref[0, r, 0], block, jnp.zeros_like(block)))
+        blocks.append(jnp.where(slot < count_ref[0, r], block, jnp.zeros_like(block)))
         weights.append(weight_ref[pick_ref[0, r, 0, slot]])
     blocks, weights = jnp.concatenate(blocks, axis=1), jnp.concatenate(weights, axis=0)
     return 0.5 * jnp.dot(blocks, weights, preferred_element_type=jnp.float32)
@@ -357,7 +357,7 @@
             flops=2 * VL * VL * 2 * LANES,
             moved=2 * 10**6,
             out_specs=[HBM],
-        )(center, rounded, column_op, remap_weights, near, far, source_rows, weight_index, counts)
+        )(center, rounded, column_op, remap_weights, near, far, source_rows, weight_index, counts.reshape(1, 2))
         return out.reshape(1, VARS, LEV, 2, LANES)
 
     in_specs = (

time: 44.5 us -> 44.4 us (level)
    unnamed x17 -> x16, local copies, waits for them, and re-layouts: 1.88 us -> 1.78 us
where the time goes in v5:
time: 44.4 us; the launch traced here: 43.8 us
  starting transfers between devices  32.3 us (73%)
  Pallas kernels  4.96 us (11%)
  waiting for transfers between devices  4.54 us (10%)
  local copies, waits for them, and re-layouts  1.78 us (4%)
    ppermute x5, starting transfers between devices, send(): return lax.ppermute(x, AXES, pairs)  32.3 us
    ppermute x5, waiting for transfers between devices, send(): return lax.ppermute(x, AXES, pairs)  4.54 us
    pallas_call x1, Pallas kernels, shards(): call(second_kernel, [((2 * VL, LANES), jnp.float32)], [VMEM] * 6 + [SMEM]...  1.9 us
    unnamed x16, local copies, waits for them, and re-layouts  1.78 us
    pallas_call x1, Pallas kernels, shards(): call(first_kernel, [((2 * VL, LANES), jnp.float32), ((VL, 2 * LANES), jnp...  1.48 us
  transfers between devices with their start and end apart: 5, of which 3 were waited for; matrix products, arithmetic and copies ran while one was open for 0% of the time, Pallas kernels for 6%

profile of v5, /device:TPU:14, one launch (start us, length us, event | category | flops | bytes accessed | tf_op | source)
XLA Modules:
  0.0 43.8 jit_solution(2343671403474741353)
XLA Ops:
  0.0 0.0 copy-start
  0.0 1.1 %copy-done = f32[1,8,72,2,128]{4,3,2,1,0:T(2,128)S(1)} copy-done((f32[1,8,72,2,128]{4,3,2,1,0:T(2,128)S(1)}, f32[1,8,72,2,128]{4,3,2,1,0:T(2,128)}, u32[]{:S(2)}) %copy-start) | copy-done | bytes 589848
  1.1 0.0 copy-start.1
  1.1 0.3 shard_map.73
  1.4 20.5 %collective-permute-start = (s16[1184,128]{1,0:T(8,128)(2,1)S(1)}, s16[1184,128]{1,0:T(8,128)(2,1)S(1)}, u32[]{:S(2)}, u32[]{:S(2)}) collective-permute-start(s16[1184,128]{1,0:T(8,128)(2,1)S(1)} %get-tuple-element.17), channel_id=1, source_target_pairs={{0,254},{1,255},{2,4},{3,5},{4,2},{5,3},{6,8},{7,9},{8,6},{9,7},{1... | collective-permute-start | bytes 909320 | tf_op jit(solution)/shard_map/ppermute | solution.py:303
  21.8 1.9 %collective-permute-start.1 = (s16[1168,128]{1,0:T(8,128)(2,1)S(1)}, s16[1168,128]{1,0:T(8,128)(2,1)S(1)}, u32[]{:S(2)}, u32[]{:S(2)}) collective-permute-start(s16[1168,128]{1,0:T(8,128)(2,1)S(1)} %get-tuple-element.18), channel_id=1, source_target_pairs={{0,2},{1,3},{2,0},{3,1},{4,6},{5,7},{6,4},{7,5},{8,10},{9,11},{10,... | collective-permute-start | bytes 897032 | tf_op jit(solution)/shard_map/ppermute | solution.py:303
  23.7 0.0 copy-start.4
  23.8 0.7 %copy-done.4 = f32[1,576]{1,0:T(1,128)S(1)} copy-done((f32[1,576]{1,0:T(1,128)S(1)}, f32[1,576]{1,0:T(1,128)}, u32[]{:S(2)}) %copy-start.4) | copy-done | bytes 2328
  24.4 0.3 shard_map.74
  24.8 0.0 copy-start.2
  24.8 0.5 %collective-permute-done.1.mate_ref = s16[1168,128]{1,0:T(8,128)(2,1)S(1)} collective-permute-done((s16[1168,128]{1,0:T(8,128)(2,1)S(1)}, s16[1168,128]{1,0:T(8,128)(2,1)S(1)}, u32[]{:S(2)}, u32[]{:S(2)}) %collective-permute-start.1) | collective-permute-done | bytes 299040 | tf_op jit(solution)/shard_map/ppermute | solution.py:303
  25.3 1.0 %collective-permute-done.link_ref = s16[1184,128]{1,0:T(8,128)(2,1)S(1)} collective-permute-done((s16[1184,128]{1,0:T(8,128)(2,1)S(1)}, s16[1184,128]{1,0:T(8,128)(2,1)S(1)}, u32[]{:S(2)}, u32[]{:S(2)}) %collective-permute-start) | collective-permute-done | bytes 303136 | tf_op jit(solution)/shard_map/ppermute | solution.py:303
  26.3 0.3 shard_map.75
  26.6 4.2 %collective-permute-start.2 = (bf16[6,8,128]{2,1,0:T(8,128)(2,1)S(1)}, bf16[6,8,128]{2,1,0:T(8,128)(2,1)S(1)}, u32[]{:S(2)}, u32[]{:S(2)}) collective-permute-start(bf16[6,8,128]{2,1,0:T(8,128)(2,1)S(1)} %get-tuple-element.22), channel_id=1, source_target_pairs={{0,512},{1,513},{2,514},{3,515},{4,516},{5,517},{6,518},{7,519},{8... | collective-permute-start | bytes 36872 | tf_op jit(solution)/shard_map/ppermute | solution.py:303
  30.8 3.3 %collective-permute-start.3 = (bf16[56,128]{1,0:T(8,128)(2,1)S(1)}, bf16[56,128]{1,0:T(8,128)(2,1)S(1)}, u32[]{:S(2)}, u32[]{:S(2)}) collective-permute-start(bf16[56,128]{1,0:T(8,128)(2,1)S(1)} %get-tuple-element.25), channel_id=1, source_target_pairs={{0,1},{1,0},{2,3},{3,2},{4,5},{5,4},{6,7},{7,6},{8,9},{9,8},{10,11... | collective-permute-start | bytes 43016 | tf_op jit(solution)/shard_map/ppermute | solution.py:303
  34.1 0.0 collective-permute-done.2.near_ref
  34.1 2.4 %collective-permute-start.4 = (bf16[12,8,128]{2,1,0:T(8,128)(2,1)S(1)}, bf16[12,8,128]{2,1,0:T(8,128)(2,1)S(1)}, u32[]{:S(2)}, u32[]{:S(2)}) collective-permute-start(bf16[12,8,128]{2,1,0:T(8,128)(2,1)S(1)} %pad_maximum_fusion), channel_id=1, source_target_pairs={{0,256},{1,257},{2,258},{3,259},{4,260},{5,261},{6,262},{7,263},{8... | collective-permute-start | bytes 73736 | tf_op jit(solution)/shard_map/ppermute | solution.py:303
  36.5 0.0 copy-done.1
  36.5 0.7 %shard_map.76 = (f32[4,576,128]{2,1,0:T(8,128)S(1)}, f32[72,128]{1,0:T(8,128)S(1)}) custom-call(f32[1152,128]{1,0:T(8,128)S(1)} %bitcast.5, s16[1184,128]{1,0:T(8,128)(2,1)S(1)} %collective-permute-done.link_ref, s16[1168,128]{1,0:T(8,128)(2,1)S(1)} %collective-permute-done.1.mate_ref, f32[576,128]{1,0:T(8,128)S(1)} %get-tuple-element.19.spread_ref, ...), custom_call_target="tpu_custom_call" | custom-call | bytes 3000000 | tf_op jit(solution)/shard_map/pallas_call | solution.py:332
  37.3 0.0 copy-start.3
  37.3 0.0 copy-start.5
  37.3 0.0 copy-start.6
  37.3 0.0 copy-start.7
  37.3 3.0 %collective-permute-done.3.recv_ref = bf16[56,128]{1,0:T(8,128)(2,1)S(1)} collective-permute-done((bf16[56,128]{1,0:T(8,128)(2,1)S(1)}, bf16[56,128]{1,0:T(8,128)(2,1)S(1)}, u32[]{:S(2)}, u32[]{:S(2)}) %collective-permute-start.3) | collective-permute-done | bytes 14368 | tf_op jit(solution)/shard_map/ppermute | solution.py:303
  40.3 0.0 copy-done.2
  40.3 1.5 %shard_map.77 = (f32[1152,128]{1,0:T(8,128)S(1)}, bf16[576,256]{1,0:T(8,128)(2,1)S(1)}) custom-call(f32[4,576,128]{2,1,0:T(8,128)S(1)} %get-tuple-element.23.rows_ref, f32[72,128]{1,0:T(8,128)S(1)} %get-tuple-element.24.full_ref, bf16[56,128]{1,0:T(8,128)(2,1)S(1)} %collective-permute-done.3.recv_ref, f32[72,128]{1,0:T(8,128)S(1)} %get-tuple-element.26.rate_ref, ...), custom_call_target="tpu_custom_call" | custom-call | flops 424673280 | bytes 2000000 | tf_op jit(solution)/shard_map/pallas_call | solution.py:338
  41.8 0.0 collective-permute-done.4.far_ref
  41.8 0.0 copy-done.3
  41.8 0.0 copy-done.5
  41.8 0.0 copy-done.6
  41.8 0.0 copy-done.7
  41.9 1.9 %shard_map.78 = f32[1152,128]{1,0:T(8,128)} custom-call(f32[1152,128]{1,0:T(8,128)S(1)} %get-tuple-element.27.center_ref, bf16[576,256]{1,0:T(8,128)(2,1)S(1)} %get-tuple-element.28.rounded_ref, bf16[1,576,576]{2,1,0:T(8,128)(2,1)S(1)} %copy-done.2, bf16[32,128,128]{2,1,0:T(8,128)(2,1)S(1)} %copy-done.3, ...), custom_call_target="tpu_custom_call" | custom-call | flops 169869312 | bytes 2000000 | tf_op jit(solution)/shard_map/pallas_call | solution.py:349
  (1 shorter events, 0.0 us)
Async XLA Ops:
  0.0 1.1 %copy-start = (f32[1,8,72,2,128]{4,3,2,1,0:T(2,128)S(1)}, f32[1,8,72,2,128]{4,3,2,1,0:T(2,128)}, u32[]{:S(2)}) copy-start(f32[1,8,72,2,128]{4,3,2,1,0:T(2,128)} %param.7) | copy-start | bytes 1769476
  1.1 35.5 %copy-start.1 = (f32[1,8,72,2,128]{4,3,2,1,0:T(2,128)S(1)}, f32[1,8,72,2,128]{4,3,2,1,0:T(2,128)}, u32[]{:S(2)}) copy-start(f32[1,8,72,2,128]{4,3,2,1,0:T(2,128)} %param.7) | copy-start | bytes 1769476
  1.4 24.9 %collective-permute-start = (s16[1184,128]{1,0:T(8,128)(2,1)S(1)}, s16[1184,128]{1,0:T(8,128)(2,1)S(1)}, u32[]{:S(2)}, u32[]{:S(2)}) collective-permute-start(s16[1184,128]{1,0:T(8,128)(2,1)S(1)} %get-tuple-element.17), channel_id=1, source_target_pairs={{0,254},{1,255},{2,4},{3,5},{4,2},{5,3},{6,8},{7,9},{8,6},{9,7},{1... | collective-permute-start | bytes 909320 | tf_op jit(solution)/shard_map/ppermute | solution.py:303
  21.8 3.5 %collective-permute-start.1 = (s16[1168,128]{1,0:T(8,128)(2,1)S(1)}, s16[1168,128]{1,0:T(8,128)(2,1)S(1)}, u32[]{:S(2)}, u32[]{:S(2)}) collective-permute-start(s16[1168,128]{1,0:T(8,128)(2,1)S(1)} %get-tuple-element.18), channel_id=1, source_target_pairs={{0,2},{1,3},{2,0},{3,1},{4,6},{5,7},{6,4},{7,5},{8,10},{9,11},{10,... | collective-permute-start | bytes 897032 | tf_op jit(solution)/shard_map/ppermute | solution.py:303
  23.7 0.7 %copy-start.4 = (f32[1,576]{1,0:T(1,128)S(1)}, f32[1,576]{1,0:T(1,128)}, u32[]{:S(2)}) copy-start(f32[1,576]{1,0:T(1,128)} %diff_ref.1) | copy-start | bytes 6916
  24.8 15.6 %copy-start.2 = (bf16[1,576,576]{2,1,0:T(8,128)(2,1)S(1)}, bf16[1,576,576]{2,1,0:T(8,128)(2,1)}, u32[]{:S(2)}) copy-start(bf16[1,576,576]{2,1,0:T(8,128)(2,1)} %op_ref.3) | copy-start | bytes 1990660
  26.6 7.5 %collective-permute-start.2 = (bf16[6,8,128]{2,1,0:T(8,128)(2,1)S(1)}, bf16[6,8,128]{2,1,0:T(8,128)(2,1)S(1)}, u32[]{:S(2)}, u32[]{:S(2)}) collective-permute-start(bf16[6,8,128]{2,1,0:T(8,128)(2,1)S(1)} %get-tuple-element.22), channel_id=1, source_target_pairs={{0,512},{1,513},{2,514},{3,515},{4,516},{5,517},{6,518},{7,519},{8... | collective-permute-start | bytes 36872 | tf_op jit(solution)/shard_map/ppermute | solution.py:303
  30.8 9.5 %collective-permute-start.3 = (bf16[56,128]{1,0:T(8,128)(2,1)S(1)}, bf16[56,128]{1,0:T(8,128)(2,1)S(1)}, u32[]{:S(2)}, u32[]{:S(2)}) collective-permute-start(bf16[56,128]{1,0:T(8,128)(2,1)S(1)} %get-tuple-element.25), channel_id=1, source_target_pairs={{0,1},{1,0},{2,3},{3,2},{4,5},{5,4},{6,7},{7,6},{8,9},{9,8},{10,11... | collective-permute-start | bytes 43016 | tf_op jit(solution)/shard_map/ppermute | solution.py:303
  34.1 7.7 %collective-permute-start.4 = (bf16[12,8,128]{2,1,0:T(8,128)(2,1)S(1)}, bf16[12,8,128]{2,1,0:T(8,128)(2,1)S(1)}, u32[]{:S(2)}, u32[]{:S(2)}) collective-permute-start(bf16[12,8,128]{2,1,0:T(8,128)(2,1)S(1)} %pad_maximum_fusion), channel_id=1, source_target_pairs={{0,256},{1,257},{2,258},{3,259},{4,260},{5,261},{6,262},{7,263},{8... | collective-permute-start | bytes 73736 | tf_op jit(solution)/shard_map/ppermute | solution.py:303
  37.3 4.6 %copy-start.3 = (bf16[32,128,128]{2,1,0:T(8,128)(2,1)S(1)}, bf16[32,128,128]{2,1,0:T(8,128)(2,1)}, u32[]{:S(2)}) copy-start(bf16[32,128,128]{2,1,0:T(8,128)(2,1)} %weight_ref.1) | copy-start | bytes 3145732
  37.3 4.6 %copy-start.5 = (s32[1,2,1,4]{3,2,1,0:T(1,128)S(1)}, s32[1,2,1,4]{3,2,1,0:T(1,128)}, u32[]{:S(2)}) copy-start(s32[1,2,1,4]{3,2,1,0:T(1,128)} %entry_ref.1) | copy-start | bytes 100
  37.3 4.6 %copy-start.6 = (s32[1,2,1,4]{3,2,1,0:T(1,128)S(1)}, s32[1,2,1,4]{3,2,1,0:T(1,128)}, u32[]{:S(2)}) copy-start(s32[1,2,1,4]{3,2,1,0:T(1,128)} %pick_ref.1) | copy-start | bytes 100
  37.3 4.6 %copy-start.7 = (s32[1,2,1]{1,2,0:T(1,128)S(1)}, s32[1,2,1]{1,2,0:T(1,128)}, u32[]{:S(2)}) copy-start(s32[1,2,1]{1,2,0:T(1,128)} %param.13) | copy-start | bytes 28
